TPU v7x, 32 devices: a whole 2x2x4 slice. The times are simulated.
32 devices in a mesh: blk: 4 (over x, core), tp: 8 (over z, y).
Axes of the slice: x: 2, y: 2, z: 4, core: 2. Of those that a mesh axis runs over, the one named last changes fastest.
Arguments:
- tokens: bfloat16 [4, 1024, 2048], P(None, 'blk'), may hold values from -6 to 6
- lengths: int32 [4, 4], replicated, may hold values from 1 to 769, 1024 in all within a row
- head_count: int32 [4, 1024], P(None, 'blk'), may hold values from 1 to 16
- width_index: int32 [4, 1024], P(None, 'blk'), may hold values from 0 to 3
- router_prob: float32 [4, 1024], P(None, 'blk'), may hold values from 0.25 to 1
- norm_gain: float32 [2048], replicated, may hold values from 0.5 to 1.5
- w_query: bfloat16 [2048, 2048], P(None, 'tp'), may hold values from -0.125 to 0.125
- w_key: bfloat16 [2048, 2048], P(None, 'tp'), may hold values from -0.125 to 0.125
- w_value: bfloat16 [2048, 2048], P(None, 'tp'), may hold values from -0.125 to 0.125
- w_out: bfloat16 [2048, 2048], P('tp'), may hold values from -1.5 to 1.5
- ln_gain: float32 [2048], replicated, may hold values from 0.5 to 1.5
- ln_bias: float32 [2048], replicated, may hold values from -3 to 3
- w_up: bfloat16 [2048, 8192], P(None, 'tp'), may hold values from -0.125 to 0.125
- w_down: bfloat16 [8192, 2048], P('tp'), may hold values from -0.0625 to 0.0625
- grad_out: bfloat16 [4, 1024, 2048], P(None, 'blk'), may hold values from -6 to 6
Outputs:
- mixed_out: bfloat16 [4, 1024, 2048], P(None, 'blk')
- grad_in: bfloat16 [4, 1024, 2048], P(None, 'blk')
- grad_norm_gain: float32 [2048], P('blk')
- grad_w_query: float32 [2048, 2048], P('blk', 'tp')
- grad_w_key: float32 [2048, 2048], P('blk', 'tp')
- grad_w_value: float32 [2048, 2048], P('blk', 'tp')
- grad_w_out: float32 [2048, 2048], P('tp', 'blk')
- grad_ln_gain: float32 [2048], P('blk')
- grad_ln_bias: float32 [2048], P('blk')
- grad_w_up: float32 [2048, 8192], P('blk', 'tp')
- grad_w_down: float32 [8192, 2048], P('tp', 'blk')
Inputs may be any that keep to these rules, and one draw needn't show every extreme that they name: `lengths`: each row sums to 1024; its longest sequence has exactly 769 rows, so it begins on the first index of blk and ends on the last. A token uses heads 0 to head_count - 1. A token uses feed-forward units 0 to (width_index + 1) * 2048 - 1.
All inputs are finite; a program needn't handle non-finite values.
Results may differ from a plain program's by a relative error of at most 0.024.
Values may be sent and summed in bfloat16 or wider, within the bound.
A program may use at most 256 MiB of HBM per device.

v0:
```python
import math

import jax
import jax.numpy as jnp
from jax import lax
from jax.sharding import PartitionSpec as P

HD = 128
FF = 8192


EPS = 1e-05
NEG = -1e30


def as_sent(array):
    return jax.tree.map(lambda a: a.astype(jnp.bfloat16) if a.dtype == jnp.float32 else a, array)


def seq_begin(lengths, rows):
    seq_ends = jnp.cumsum(lengths, axis=1)
    past_end = rows[None, :, None] >= seq_ends[:, None, :]
    return jnp.sum(jnp.where(past_end, lengths[:, None, :], 0), axis=2)


def turn_table(positions, dim_size):
    half_dim = dim_size // 2
    frequency = jnp.exp(jnp.arange(half_dim, dtype=jnp.float32) * (-math.log(10000.0) / half_dim))
    angles = positions.astype(jnp.float32)[..., None] * frequency
    return (jnp.cos(angles)[..., None, :], jnp.sin(angles)[..., None, :])


def rotate(values_in, cos_table, sine_table):
    half_dim = values_in.shape[-1] // 2
    first_half = values_in[..., :half_dim]
    second_half = values_in[..., half_dim:]
    return jnp.concatenate(
        [
            first_half * cos_table - second_half * sine_table,
            first_half * sine_table + second_half * cos_table,
        ],
        axis=-1,
    )


def rotate_back(grad_rot, cos_table, sine_table):
    half_dim = grad_rot.shape[-1] // 2
    first_half = grad_rot[..., :half_dim]
    second_half = grad_rot[..., half_dim:]
    return jnp.concatenate(
        [
            first_half * cos_table + second_half * sine_table,
            second_half * cos_table - first_half * sine_table,
        ],
        axis=-1,
    )


def allowed_pairs(q_rows, q_begin, k_rows):
    causal_ok = k_rows[None, None, :] <= q_rows[None, :, None]
    inside_seq = k_rows[None, None, :] >= q_begin[:, :, None]
    return (causal_ok & inside_seq)[:, None]


def pair_grads(
    q_block, grad_block, logsum, row_delta, q_rows, q_begin, k_block, v_block, k_rows, score_scale
):
    raw_score = jnp.einsum("mqhd,mkhd->mhqk", q_block, k_block, preferred_element_type=jnp.float32)
    allowed = allowed_pairs(q_rows, q_begin, k_rows)
    prob_rows = jnp.where(allowed, jnp.exp(raw_score * score_scale - logsum[..., None]), 0.0)
    grad_prob = jnp.einsum(
        "mqhd,mkhd->mhqk", grad_block, v_block, preferred_element_type=jnp.float32
    )
    grad_score = (prob_rows * (grad_prob - row_delta[..., None]) * score_scale).astype(jnp.bfloat16)
    result = []
    result.append(
        jnp.einsum("mhqk,mkhd->mqhd", grad_score, k_block, preferred_element_type=jnp.float32)
    )
    result.append(
        jnp.einsum("mhqk,mqhd->mkhd", grad_score, q_block, preferred_element_type=jnp.float32)
    )
    result.append(
        jnp.einsum(
            "mhqk,mqhd->mkhd",
            prob_rows.astype(jnp.bfloat16),
            grad_block,
            preferred_element_type=jnp.float32,
        )
    )
    return tuple(result)


def local(
    tokens,
    lengths,
    head_count,
    width_index,
    router_prob,
    norm_gain,
    w_query,
    w_key,
    w_value,
    w_out,
    ln_gain,
    ln_bias,
    w_up,
    w_down,
    grad_out,
):
    batches, rows_dev, features = tokens.shape
    local_heads = w_query.shape[1] // HD
    unit_count = w_up.shape[1]
    blocks = lax.axis_size("blk")
    first_row = lax.axis_index("blk") * rows_dev
    last_row = first_row + rows_dev - 1
    local_rows = first_row + jnp.arange(rows_dev, dtype=jnp.int32)
    local_begin = seq_begin(lengths, local_rows)
    cos_table, sine_table = turn_table(local_rows[None, :] - local_begin, HD)
    score_scale = 1.0 / math.sqrt(HD)
    head_ids = lax.axis_index("tp") * local_heads + jnp.arange(local_heads, dtype=jnp.int32)
    head_mask = (head_ids[None, None, :] < head_count[:, :, None]).astype(jnp.float32)
    unit_ids = lax.axis_index("tp") * unit_count + jnp.arange(unit_count, dtype=jnp.int32)
    unit_mask = (unit_ids[None, None, :] < (width_index[:, :, None] + 1) * (FF // 4)).astype(
        jnp.float32
    )
    block_shape = (batches, rows_dev, local_heads, HD)
    inputs = tokens.astype(jnp.float32)
    inv_rms = lax.rsqrt(jnp.mean(inputs * inputs, axis=-1, keepdims=True) + EPS)
    scaled = inputs * inv_rms
    normed = (scaled * norm_gain).astype(jnp.bfloat16)

    def project(matrix):
        return jnp.einsum(
            "mtd,de->mte", normed, matrix, preferred_element_type=jnp.float32
        ).reshape(block_shape)

    query_local = rotate(project(w_query), cos_table, sine_table).astype(jnp.bfloat16)
    key_local = rotate(project(w_key), cos_table, sine_table).astype(jnp.bfloat16)
    value_local = project(w_value).astype(jnp.bfloat16)
    start_state = (
        jnp.full((batches, local_heads, rows_dev), NEG, jnp.float32),
        jnp.zeros((batches, local_heads, rows_dev), jnp.float32),
        jnp.zeros((batches, local_heads, rows_dev, HD), jnp.float32),
    )
    key_piece = lax.all_gather(key_local, "blk", axis=1, tiled=True)
    value_piece = lax.all_gather(value_local, "blk", axis=1, tiled=True)
    k_rows = jnp.arange(key_piece.shape[1], dtype=jnp.int32)

    def attend_compute_part(state_now):
        row_max, row_sum, weighted = state_now
        raw_score = jnp.einsum(
            "mqhd,mkhd->mhqk", query_local, key_piece, preferred_element_type=jnp.float32
        )
        allowed = allowed_pairs(local_rows, local_begin, k_rows)
        score = jnp.where(allowed, raw_score * score_scale, NEG)
        new_max = jnp.maximum(row_max, jnp.max(score, axis=-1))
        weights = jnp.where(allowed, jnp.exp(score - new_max[..., None]), 0.0)
        new_sum = jnp.sum(weights, axis=-1)
        new_weighted = jnp.einsum(
            "mhqk,mkhd->mhqd",
            weights.astype(jnp.bfloat16),
            value_piece,
            preferred_element_type=jnp.float32,
        )
        return (new_max, new_sum, new_weighted)

    row_max, row_sum, weighted = lax.cond(
        jnp.int32(0) > last_row, lambda state_now: state_now, attend_compute_part, start_state
    )
    logsum = row_max + jnp.log(row_sum)
    attended = jnp.transpose(weighted / row_sum[..., None], (0, 2, 1, 3)) * head_mask[..., None]
    heads_out = attended.astype(jnp.bfloat16).reshape(batches, rows_dev, local_heads * HD)
    router_col = router_prob[..., None]
    upstream = grad_out.astype(jnp.float32)
    branch = lax.psum(
        jnp.einsum("mte,ed->mtd", heads_out, w_out, preferred_element_type=jnp.float32).astype(
            jnp.bfloat16
        ),
        "tp",
    ).astype(jnp.float32)
    residual = inputs + branch
    center = residual - jnp.mean(residual, axis=-1, keepdims=True)
    inv_std = lax.rsqrt(jnp.mean(center * center, axis=-1, keepdims=True) + EPS)
    normal_ln = center * inv_std
    lifted = (normal_ln * ln_gain + ln_bias).astype(jnp.bfloat16)
    hidden = jnp.einsum("mtd,df->mtf", lifted, w_up, preferred_element_type=jnp.float32)
    active = jnp.maximum(hidden, 0.0)
    squared = (active * active * unit_mask).astype(jnp.bfloat16)
    feed_out = lax.psum(
        jnp.einsum("mtf,fd->mtd", squared, w_down, preferred_element_type=jnp.float32).astype(
            jnp.bfloat16
        ),
        "tp",
    ).astype(jnp.float32)
    mixed_out = (residual + router_col * feed_out).astype(jnp.bfloat16)
    grad_feed = (router_col * upstream).astype(jnp.bfloat16)
    grad_down = jnp.einsum("mtf,mtd->fd", squared, grad_feed, preferred_element_type=jnp.float32)
    grad_hidden = (
        jnp.einsum("mtd,fd->mtf", grad_feed, w_down, preferred_element_type=jnp.float32)
        * unit_mask
        * 2.0
        * active
    ).astype(jnp.bfloat16)
    grad_upw = jnp.einsum("mtd,mtf->df", lifted, grad_hidden, preferred_element_type=jnp.float32)
    grad_lifted = lax.psum(
        jnp.einsum("mtf,df->mtd", grad_hidden, w_up, preferred_element_type=jnp.float32).astype(
            jnp.bfloat16
        ),
        "tp",
    ).astype(jnp.float32)
    ln_gain_part = jnp.sum(grad_lifted * normal_ln, axis=(0, 1))
    ln_bias_part = jnp.sum(grad_lifted, axis=(0, 1))
    grad_norm_ln = grad_lifted * ln_gain
    grad_resid = upstream + inv_std * (
        grad_norm_ln
        - jnp.mean(grad_norm_ln, axis=-1, keepdims=True)
        - normal_ln * jnp.mean(grad_norm_ln * normal_ln, axis=-1, keepdims=True)
    )
    grad_branch = grad_resid.astype(jnp.bfloat16)
    grad_outw = jnp.einsum(
        "mte,mtd->ed", heads_out, grad_branch, preferred_element_type=jnp.float32
    )
    grad_heads = (
        jnp.einsum("mtd,ed->mte", grad_branch, w_out, preferred_element_type=jnp.float32)
        .astype(jnp.bfloat16)
        .reshape(block_shape)
    )
    grad_block = grad_heads * head_mask[..., None].astype(jnp.bfloat16)
    row_delta = jnp.sum(grad_block.astype(jnp.float32) * attended, axis=-1)
    delta_heads = jnp.transpose(row_delta, (0, 2, 1))
    key_all, value_all = (
        lax.all_gather(key_local, "blk", axis=1, tiled=True),
        lax.all_gather(value_local, "blk", axis=1, tiled=True),
    )

    def key_step(grad_query, piece_index):
        row_start = piece_index * rows_dev
        key_piece = lax.dynamic_slice_in_dim(key_all, row_start, rows_dev, 1)
        value_piece = lax.dynamic_slice_in_dim(value_all, row_start, rows_dev, 1)
        k_rows = row_start + jnp.arange(rows_dev, dtype=jnp.int32)

        def key_compute_part(running):
            pair_parts = pair_grads(
                query_local,
                grad_block,
                logsum,
                delta_heads,
                local_rows,
                local_begin,
                key_piece,
                value_piece,
                k_rows,
                score_scale,
            )
            return (running + pair_parts[0], pair_parts[1:])

        def skip_part(running):
            zero_block = jnp.zeros(block_shape, jnp.float32)
            return (running, (zero_block, zero_block))

        return lax.cond(row_start > last_row, skip_part, key_compute_part, grad_query)

    grad_query, key_terms = lax.scan(
        key_step, jnp.zeros(block_shape, jnp.float32), jnp.arange(blocks, dtype=jnp.int32)
    )
    summed_keys, summed_values = jax.tree.map(
        lambda part: part.astype(jnp.float32),
        lax.psum_scatter(as_sent(key_terms), "blk", scatter_dimension=0, tiled=True),
    )
    grad_keys = summed_keys[0]
    grad_values = summed_values[0]
    flat_shape = (batches, rows_dev, local_heads * HD)
    grad_q_pre = (
        rotate_back(grad_query, cos_table, sine_table).astype(jnp.bfloat16).reshape(flat_shape)
    )
    grad_k_pre = (
        rotate_back(grad_keys, cos_table, sine_table).astype(jnp.bfloat16).reshape(flat_shape)
    )
    grad_v_pre = grad_values.astype(jnp.bfloat16).reshape(flat_shape)
    grad_wq = jnp.einsum("mtd,mte->de", normed, grad_q_pre, preferred_element_type=jnp.float32)
    grad_wk = jnp.einsum("mtd,mte->de", normed, grad_k_pre, preferred_element_type=jnp.float32)
    grad_wv = jnp.einsum("mtd,mte->de", normed, grad_v_pre, preferred_element_type=jnp.float32)
    normed_part = (
        jnp.einsum("mte,de->mtd", grad_q_pre, w_query, preferred_element_type=jnp.float32)
        + jnp.einsum("mte,de->mtd", grad_k_pre, w_key, preferred_element_type=jnp.float32)
        + jnp.einsum("mte,de->mtd", grad_v_pre, w_value, preferred_element_type=jnp.float32)
    )
    grad_normed = lax.psum(normed_part.astype(jnp.bfloat16), "tp").astype(jnp.float32)
    gain_part = jnp.sum(grad_normed * scaled, axis=(0, 1))
    grad_scaled = grad_normed * norm_gain
    grad_input = grad_resid + inv_rms * (
        grad_scaled - scaled * jnp.mean(grad_scaled * scaled, axis=-1, keepdims=True)
    )
    grad_in = grad_input.astype(jnp.bfloat16)
    reduced = (
        lax.psum_scatter(
            gain_part.astype(jnp.bfloat16), "blk", scatter_dimension=0, tiled=True
        ).astype(jnp.float32),
        lax.psum_scatter(
            grad_wq.astype(jnp.bfloat16), "blk", scatter_dimension=0, tiled=True
        ).astype(jnp.float32),
        lax.psum_scatter(
            grad_wk.astype(jnp.bfloat16), "blk", scatter_dimension=0, tiled=True
        ).astype(jnp.float32),
        lax.psum_scatter(
            grad_wv.astype(jnp.bfloat16), "blk", scatter_dimension=0, tiled=True
        ).astype(jnp.float32),
        lax.psum_scatter(
            grad_outw.astype(jnp.bfloat16), "blk", scatter_dimension=1, tiled=True
        ).astype(jnp.float32),
        lax.psum_scatter(
            ln_gain_part.astype(jnp.bfloat16), "blk", scatter_dimension=0, tiled=True
        ).astype(jnp.float32),
        lax.psum_scatter(
            ln_bias_part.astype(jnp.bfloat16), "blk", scatter_dimension=0, tiled=True
        ).astype(jnp.float32),
        lax.psum_scatter(
            grad_upw.astype(jnp.bfloat16), "blk", scatter_dimension=0, tiled=True
        ).astype(jnp.float32),
        lax.psum_scatter(
            grad_down.astype(jnp.bfloat16), "blk", scatter_dimension=1, tiled=True
        ).astype(jnp.float32),
    )
    return (
        mixed_out,
        grad_in,
        reduced[0],
        reduced[1],
        reduced[2],
        reduced[3],
        reduced[4],
        reduced[5],
        reduced[6],
        reduced[7],
        reduced[8],
    )


def solution(mesh):
    return jax.shard_map(
        local,
        mesh=mesh,
        in_specs=(
            P(None, "blk", None),
            P(),
            P(None, "blk"),
            P(None, "blk"),
            P(None, "blk"),
            P(),
            P(None, "tp"),
            P(None, "tp"),
            P(None, "tp"),
            P("tp", None),
            P(),
            P(),
            P(None, "tp"),
            P("tp", None),
            P(None, "blk", None),
        ),
        out_specs=(
            P(None, "blk", None),
            P(None, "blk", None),
            P("blk"),
            P("blk", "tp"),
            P("blk", "tp"),
            P("blk", "tp"),
            P("tp", "blk"),
            P("blk"),
            P("blk"),
            P("blk", "tp"),
            P("tp", "blk"),
        ),
        check_vma=False,
    )
```

profile of v0, /device:TPU:0, one launch (start us, length us, event | category | flops | bytes accessed | tf_op | source)
XLA Modules:
  0.0 1080.3 jit_solution(15034376272284674943)
XLA Ops:
  9.1 3.3 fusion.40
  12.5 2.7 fusion.86
  16.5 1.4 copy.134
  17.9 4.0 fusion.82
  22.9 2.4 copy.135
  25.3 2.4 copy.136
  27.6 1.9 multiply_cosine_fusion
  30.3 3.1 subtract_convert_fusion.2
  33.4 1.1 pad_maximum_fusion.1
  34.6 4.1 convolution_convert_fusion.1
  40.3 1.1 pad_maximum_fusion
  41.4 18.5 %all-gather.3.cloned.1.call-done = bf16[4,1024,2,128]{3,1,2,0:T(8,128)(2,1)} async-done(((bf16[4,256,2,128]{3,1,2,0:T(8,128)(2,1)}), bf16[4,1024,2,128]{3,1,2,0:T(8,128)(2,1)}) %all-gather.3.cloned.1.call-update) | async-done | bytes 2097168 | tf_op jit(solution)/shard_map/all_gather | solution.py:145
  60.0 24.7 %all-gather.5.cloned.1.call-done = bf16[4,1024,2,128]{3,1,2,0:T(8,128)(2,1)} async-done(((bf16[4,256,2,128]{3,1,2,0:T(8,128)(2,1)}), bf16[4,1024,2,128]{3,1,2,0:T(8,128)(2,1)}) %all-gather.5.cloned.1.call-update) | async-done | bytes 2097168 | tf_op jit(solution)/shard_map/all_gather | solution.py:146
  84.7 10.9 %conditional.2 = (f32[4,2,256]{2,1,0:T(2,128)S(1)}, f32[4,2,256]{2,1,0:T(2,128)S(1)}, f32[4,2,256]{2,1,0:T(2,128)S(1)}, f32[4,2,256,128]{2,3,1,0:T(8,128)S(1)}) conditional(s32[]{:T(128)} %convert_element_type.194, (s32[1024]{0:T(1024)S(1)}, s32[256]{0:T(256)S(1)}, s32[1024]{0:T(1024)S(1)}, s32[4,256]{1,0:T(4,128)S(1)}, ...), branch_computations={%region_3.6_spmd, %region_6.7_spmd} | conditional | flops 1103362048 | bytes 44119100 | solution.py:167
  85.7 3.7 fusion.2
  89.4 3.1 fusion.4
  92.5 3.0 fusion.5
  96.5 3.3 convolution_convert_fusion
  100.1 156.2 %all-reduce.9.cloned.1.call-done = bf16[4,256,2048]{2,1,0:T(8,128)(2,1)} async-done(((bf16[4,256,2048]{2,1,0:T(8,128)(2,1)}), bf16[4,256,2048]{2,1,0:T(8,128)(2,1)}) %all-reduce.9.cloned.1.call-update) | async-done | bytes 4194320 | tf_op jit(solution)/shard_map/psum | solution.py:175
  256.3 4.8 fusion.41
  261.1 1.1 copy-done.6
  262.2 1.8 multiply_reduce_fusion
  264.4 4.7 fusion.52
  269.2 6.1 fusion.45
  275.3 7.7 fusion.54
  283.3 155.2 %all-reduce.11.cloned.1.call-done = bf16[4,256,2048]{2,1,0:T(8,128)(2,1)} async-done(((bf16[4,256,2048]{2,1,0:T(8,128)(2,1)}), bf16[4,256,2048]{2,1,0:T(8,128)(2,1)}) %all-reduce.11.cloned.1.call-update) | async-done | bytes 4194320 | tf_op jit(solution)/shard_map/psum | solution.py:205
  438.5 7.5 fusion.36
  446.8 6.1 fusion.73
  453.5 20.7 %while.18 = (s32[]{:T(128)}, f32[4,256,2,128]{3,1,2,0:T(8,128)S(1)}, bf16[4,4,256,2,128]{4,2,3,1,0:T(8,128)(2,1)}, bf16[4,4,256,2,128]{2,4,3,1,0:T(8,128)(2,1)},...) while((s32[]{:T(128)}, ...), condition=%wide.region_18.19_spmd.clone, body=%wide.region_15.18_spmd.clone.sunk | while | flops 676135424 | bytes 20084072 | solution.py:263
  454.8 7.5 conditional.5
  455.2 1.9 bitcast_select_fusion
  457.1 1.5 fusion.12
  458.6 1.8 fusion.13
  460.4 1.5 convolution_bitcast_fusion.1
  475.2 9.3 fusion.65
  485.1 11.6 %bitcast_convert_fusion.1 = bf16[2048,1024]{1,0:T(8,128)(2,1)} fusion(bf16[4,256,1024]{2,1,0:T(8,128)(2,1)} %fusion.45, f32[2048]{0:T(1024)S(1)} %copy-done.34, f32[2048]{0:T(1024)S(1)} %copy-done.27, f32[4,256]{1,0:T(4,128)S(1)} %add_rsqrt_fusion, f32[4,256]{1,0:T(4,128)S(1)} %broadcast_multiply_fusion.4, ...), kind=kOutput, calls=%fused_computation.64 | convolution fusion | flops 4313841664 | bytes 14704640 | tf_op jit(solution)/shard_map/mtd,mtf->df/dot_general | solution.py:204
  496.7 10.2 bitcast_convert_fusion
  507.2 19.2 %reduce-scatter.9.cloned.1.call-done = bf16[1,4,256,2,128]{4,2,3,1,0:T(8,128)(2,1)} async-done(((bf16[4,4,256,2,128]{4,2,3,1,0:T(8,128)(2,1)}), bf16[1,4,256,2,128]{4,2,3,1,0:T(8,128)(2,1)}) %reduce-scatter.9.cloned.1.call-update) | async-done | bytes 524304 | tf_op jit(solution)/shard_map/reduce_scatter | solution.py:268
  526.4 1.3 bitcast_convert_fusion.2
  529.5 3.0 fusion.63
  532.5 5.1 fusion.62
  537.7 23.3 %reduce-scatter.11.cloned.1.call-done = bf16[1,4,256,2,128]{2,4,3,1,0:T(8,128)(2,1)} async-done(((bf16[4,4,256,2,128]{2,4,3,1,0:T(8,128)(2,1)}), bf16[1,4,256,2,128]{2,4,3,1,0:T(8,128)(2,1)}) %reduce-scatter.11.cloned.1.call-update) | async-done | bytes 524304 | tf_op jit(solution)/shard_map/reduce_scatter | solution.py:268
  561.0 4.9 fusion.64
  566.2 10.3 fusion.57
  576.5 1.3 fusion.80
  577.9 1.3 fusion.84
  579.2 3.4 add_convert_fusion
  584.5 2.9 reduce_sum.121
  587.4 1.1 reduce-scatter.19.cloned.1.call-done
  588.4 1.8 convert_element_type.234
  590.2 45.4 %reduce-scatter.21.cloned.1.call-done = bf16[512,1024]{1,0:T(8,128)(2,1)} async-done(((bf16[2048,1024]{1,0:T(8,128)(2,1)}), bf16[512,1024]{1,0:T(8,128)(2,1)}) %reduce-scatter.21.cloned.1.call-update) | async-done | bytes 1048592 | tf_op jit(solution)/shard_map/reduce_scatter | solution.py:317
  635.7 2.8 convert_element_type.239
  638.5 44.3 %reduce-scatter.23.cloned.1.call-done = bf16[1024,512]{1,0:T(8,128)(2,1)} async-done(((bf16[1024,2048]{1,0:T(8,128)(2,1)}), bf16[1024,512]{1,0:T(8,128)(2,1)}) %reduce-scatter.23.cloned.1.call-update) | async-done | bytes 1048592 | tf_op jit(solution)/shard_map/reduce_scatter | solution.py:320
  682.7 2.8 convert_element_type.241
  685.6 24.6 %reduce-scatter.15.cloned.1.call-done = bf16[512,256]{1,0:T(8,128)(2,1)} async-done(((bf16[2048,256]{1,0:T(8,128)(2,1)}), bf16[512,256]{1,0:T(8,128)(2,1)}) %reduce-scatter.15.cloned.1.call-update) | async-done | bytes 262160 | tf_op jit(solution)/shard_map/reduce_scatter | solution.py:302
  710.2 1.8 convert_element_type.230
  712.0 25.7 %reduce-scatter.13.cloned.1.call-done = bf16[512,256]{1,0:T(8,128)(2,1)} async-done(((bf16[2048,256]{1,0:T(8,128)(2,1)}), bf16[512,256]{1,0:T(8,128)(2,1)}) %reduce-scatter.13.cloned.1.call-update) | async-done | bytes 262160 | tf_op jit(solution)/shard_map/reduce_scatter | solution.py:299
  737.7 1.8 convert_element_type.228
  739.4 25.7 %reduce-scatter.17.cloned.1.call-done = bf16[512,256]{1,0:T(8,128)(2,1)} async-done(((bf16[2048,256]{1,0:T(8,128)(2,1)}), bf16[512,256]{1,0:T(8,128)(2,1)}) %reduce-scatter.17.cloned.1.call-update) | async-done | bytes 262160 | tf_op jit(solution)/shard_map/reduce_scatter | solution.py:305
  765.1 1.8 convert_element_type.232
  766.9 274.0 %all-reduce.13.cloned.1.call-done = (bf16[4,256,2048]{2,1,0:T(8,128)(2,1)}, bf16[4,256,2048]{2,1,0:T(8,128)(2,1)}) async-done(((bf16[4,256,2048]{2,1,0:T(8,128)(2,1)}, bf16[4,256,2048]{2,1,0:T(8,128)(2,1)}), (bf16[4,256,2048]{2,1,0:T(8,128)(2,1)}, bf16[4,256,2048]{2,1,0:T(8,128)(2,1)})) %all-reduce.13.cloned.1.call-update) | async-done | bytes 8388624 | tf_op jit(solution)/shard_map/psum | solution.py:189
  1040.9 5.5 fusion.39
  1046.4 11.1 %all-reduce.4 = (bf16[2048]{0:T(1024)(128)(2,1)S(1)}, bf16[2048]{0:T(1024)(128)(2,1)S(1)}, bf16[2048]{0:T(1024)(128)(2,1)S(1)}) all-reduce(bf16[2048]{0:T(1024)(128)(2,1)S(1)} %get-tuple-element.334, bf16[2048]{0:T(1024)(128)(2,1)S(1)} %get-tuple-element.332, ...), channel_id=4, replica_groups=mesh['blk'=4,'tp'=8] {'blk'}, use_global_device_ids=true, to_apply=%region_24.25.clone | all-reduce | flops 6144 | bytes 24576
  1059.5 14.0 %fusion.31 = (bf16[4,256,2048]{2,1,0:T(8,128)(2,1)}, bf16[4,256,2048]{2,1,0:T(8,128)(2,1)}) fusion(bf16[4,256,2048]{2,1,0:T(8,128)(2,1)} %get-tuple-element.366, bf16[4,256,2048]{2,1,0:T(8,128)(2,1)} %param.21, f32[4,256]{1,0:T(4,128)S(1)} %broadcast_multiply_fusion.1, f32[2048]{0:T(1024)S(1)} %copy-done.28, f32[4,256]{1,0:T(4,128)S(1)} %add_rsqrt_fusion.1, ...), kind=kLoop, calls=%fused_computation.53 | loop fusion | flops 52428800 | bytes 33599488 | tf_op jit(solution)/shard_map/convert_element_type | solution.py:294
  (168 shorter events, 29.7 us)
Async XLA Ops:
  7.2 89.3 %copy-start = (bf16[256,2048]{1,0:T(8,128)(2,1)S(1)}, bf16[256,2048]{1,0:T(8,128)(2,1)}, u32[]{:S(2)}) copy-start(bf16[256,2048]{1,0:T(8,128)(2,1)} %param.30) | copy-start | bytes 3145732
  7.2 5.3 copy-start.28
  7.2 52.8 %all-gather.3.cloned.1.call-start = ((), (), s32[]{:S(2)}) async-start(), calls=%async_computation.8 | async-start | bytes 2621440 | tf_op jit(solution)/shard_map/all_gather | solution.py:145
  8.2 4.3 copy-start.2
  29.5 0.8 copy-start.9
  29.5 3.9 copy-start.11
  34.5 5.8 copy-start.19
  34.5 5.8 copy-start.20
  34.5 6.9 copy-start.31
  34.5 50.2 %all-gather.5.cloned.1.call-start = ((), (), s32[]{:S(2)}) async-start(), calls=%async_computation.9 | async-start | bytes 2621440 | tf_op jit(solution)/shard_map/all_gather | solution.py:146
  39.7 216.6 %all-reduce.9.cloned.1.call-start = ((), (), s32[]{:S(2)}) async-start(), calls=%async_computation.10 | async-start | bytes 8388608 | tf_op jit(solution)/shard_map/psum | solution.py:175
  89.4 3.1 copy-start.14
  95.7 0.8 copy-start.21
  96.5 3.6 copy-start.30
  99.8 338.6 %all-reduce.11.cloned.1.call-start = ((), (), s32[]{:S(2)}) async-start(), calls=%async_computation.11 | async-start | bytes 8388608 | tf_op jit(solution)/shard_map/psum | solution.py:205
  256.3 4.8 copy-start.3
  256.3 5.9 copy-start.6
  262.2 1.8 copy-start.27
  262.2 2.2 copy-start.32
  262.2 2.2 copy-start.34
  264.4 4.7 copy-start.13
  264.4 4.8 copy-start.29
  264.4 4.8 copy-start.33
  269.2 6.1 copy-start.36
  283.0 243.4 %reduce-scatter.9.cloned.1.call-start = ((), (), s32[]{:S(2)}) async-start(), calls=%async_computation.12 | async-start | bytes 2621440 | tf_op jit(solution)/shard_map/reduce_scatter | solution.py:268
  438.5 7.6 copy-start.4
  438.5 7.6 copy-start.7
  438.5 8.3 copy-start.8
  474.2 1.0 copy-start.22
  474.2 86.8 %reduce-scatter.11.cloned.1.call-start = ((), (), s32[]{:S(2)}) async-start(), calls=%async_computation.13 | async-start | bytes 2621440 | tf_op jit(solution)/shard_map/reduce_scatter | solution.py:268
  474.8 113.6 %reduce-scatter.19.cloned.1.call-start = ((), (), s32[]{:S(2)}) async-start(), calls=%async_computation.17 | async-start | bytes 1310720 | tf_op jit(solution)/shard_map/reduce_scatter | solution.py:308
  484.6 151.1 %reduce-scatter.21.cloned.1.call-start = ((), (), s32[]{:S(2)}) async-start(), calls=%async_computation.18 | async-start | bytes 5242880 | tf_op jit(solution)/shard_map/reduce_scatter | solution.py:317
  496.6 186.1 %reduce-scatter.23.cloned.1.call-start = ((), (), s32[]{:S(2)}) async-start(), calls=%async_computation.19 | async-start | bytes 5242880 | tf_op jit(solution)/shard_map/reduce_scatter | solution.py:320
  506.9 20.7 %copy-start.10 = (f32[4,256,64]{2,1,0:T(8,128)S(1)}, f32[4,256,64]{2,1,0:T(8,128)}, u32[]{:S(2)}) copy-start(f32[4,256,64]{2,1,0:T(8,128)} %copy-done.9) | copy-start | bytes 786436
  506.9 20.7 %copy-start.12 = (f32[4,256,64]{2,1,0:T(8,128)S(1)}, f32[4,256,64]{2,1,0:T(8,128)}, u32[]{:S(2)}) copy-start(f32[4,256,64]{2,1,0:T(8,128)} %copy-done.11) | copy-start | bytes 786436
  507.0 203.2 %reduce-scatter.15.cloned.1.call-start = ((), (), s32[]{:S(2)}) async-start(), calls=%async_computation.15 | async-start | bytes 1310720 | tf_op jit(solution)/shard_map/reduce_scatter | solution.py:302
  526.4 3.1 copy-start.5
  528.5 0.8 copy-start.15
  528.5 1.0 copy-start.17
  532.5 205.2 %reduce-scatter.13.cloned.1.call-start = ((), (), s32[]{:S(2)}) async-start(), calls=%async_computation.14 | async-start | bytes 1310720 | tf_op jit(solution)/shard_map/reduce_scatter | solution.py:299
  537.6 227.5 %reduce-scatter.17.cloned.1.call-start = ((), (), s32[]{:S(2)}) async-start(), calls=%async_computation.16 | async-start | bytes 1310720 | tf_op jit(solution)/shard_map/reduce_scatter | solution.py:305
  565.9 10.6 copy-start.16
  565.9 10.6 copy-start.18
  565.9 10.6 copy-start.23
  565.9 475.0 %all-reduce.13.cloned.1.call-start = ((), (), s32[]{:S(2)}) async-start(), calls=%async_computation.20 | async-start | bytes 16777216 | tf_op jit(solution)/shard_map/psum | solution.py:189
  576.5 1.3 copy-start.24
  577.9 1.3 copy-start.25
  577.9 1.3 copy-start.26
  582.6 0.7 copy-start.35
  1059.5 14.0 %copy-start.1 = (bf16[256,2048]{1,0:T(8,128)(2,1)S(1)}, bf16[256,2048]{1,0:T(8,128)(2,1)}, u32[]{:S(2)}) copy-start(bf16[256,2048]{1,0:T(8,128)(2,1)} %param.30) | copy-start | bytes 3145732
Sparse Core Ops, SparseCore 0:
  34.6 25.3 all-gather.2
  62.1 22.5 all-gather.4
  100.0 156.2 all-reduce.8
  283.1 155.3 all-reduce.10
  474.3 52.0 reduce-scatter.8
  529.5 31.4 reduce-scatter.10
  563.5 24.8 reduce-scatter.18
  591.1 44.5 reduce-scatter.20
  638.2 44.4 reduce-scatter.22
  685.3 24.8 reduce-scatter.14
  712.7 24.8 reduce-scatter.12
  740.2 24.8 reduce-scatter.16
  769.8 271.0 all-reduce.12
where the time goes:
time: 1090 us; the launch traced here: 1080 us
  waiting for transfers between devices  839 us (77%)
  matrix products  113 us (10%)
  other arithmetic  70.5 us (6%)
  local copies, waits for them, and re-layouts  26.5 us (2%)
  between operations  15.3 us (1%)
  blocking collectives  11.1 us (1%)
    psum x1, waiting for transfers between devices, local(): lax.psum(jnp.einsum('mtf,fd->mtd', squared, w_down, preferred_element_typ...  274 us
    psum x1, waiting for transfers between devices, local(): lax.psum(jnp.einsum('mte,ed->mtd', heads_out, w_out, preferred_element_ty...  156 us
    psum x1, waiting for transfers between devices, local(): lax.psum(jnp.einsum('mtf,df->mtd', grad_hidden, w_up, preferred_element_t...  155 us
    reduce_scatter x1, waiting for transfers between devices, local(): lax.psum_scatter(grad_upw.astype(jnp.bfloat16), 'blk', scatter_dimension=...  45.4 us
    reduce_scatter x1, waiting for transfers between devices, local(): lax.psum_scatter(grad_down.astype(jnp.bfloat16), 'blk', scatter_dimension...  44.3 us
    reduce_scatter x2, waiting for transfers between devices, local(): lax.psum_scatter(as_sent(key_terms), 'blk', scatter_dimension=0, tiled=True)  42.5 us
    reduce_scatter x1, waiting for transfers between devices, local(): lax.psum_scatter(grad_wq.astype(jnp.bfloat16), 'blk', scatter_dimension=0...  25.7 us
    reduce_scatter x1, waiting for transfers between devices, local(): lax.psum_scatter(grad_wv.astype(jnp.bfloat16), 'blk', scatter_dimension=0...  25.7 us
  transfers between devices with their start and end apart: 13, of which 13 were waited for; matrix products, arithmetic and copies ran while one was open for 8% of the time, Pallas kernels for 0%

commit v1 on v0

--- a/solution.py
+++ b/solution.py
@@ -1,8 +1,11 @@
+import functools
 import math
 
 import jax
 import jax.numpy as jnp
 from jax import lax
+from jax.experimental import pallas as pl
+from jax.experimental.pallas import tpu as pltpu
 from jax.sharding import PartitionSpec as P
 
 HD = 128
@@ -11,6 +14,585 @@
 
 EPS = 1e-05
 NEG = -1e30
+CHUNK_ROWS = 128
+CUT = 1280
+VMEM_LIMIT = 60 * 2**20
+
+
+MESH = pl.DeviceIdType.MESH
+VMEM = pltpu.VMEM
+LANE = 128
+
+
+def remote(src, dst, send, recv, device):
+    return pltpu.make_async_remote_copy(
+        src_ref=src, dst_ref=dst, send_sem=send, recv_sem=recv, device_id=device, device_id_type=MESH
+    )
+
+
+class Place:
+    def __init__(self, lines):
+        blk, tp = lax.axis_index("blk"), lax.axis_index("tp")
+        self.lines, self.tp = lines, tp
+        self.z, self.y = tp // 2, tp % 2
+        self.other = 1 - self.y
+        self.across = (blk, self.z * 2 + self.other)
+        self.right = (blk, jnp.minimum(self.z + 1, lines - 1) * 2 + self.y)
+        self.left = (blk, jnp.maximum(self.z - 1, 0) * 2 + self.y)
+        self.has_right, self.has_left = self.z < lines - 1, self.z > 0
+
+    def greet(self):
+        barrier = pltpu.get_barrier_semaphore()
+        pl.semaphore_signal(barrier, inc=1, device_id=self.across, device_id_type=MESH)
+
+        @pl.when(self.has_right)
+        def _():
+            pl.semaphore_signal(barrier, inc=1, device_id=self.right, device_id_type=MESH)
+
+        @pl.when(self.has_left)
+        def _():
+            pl.semaphore_signal(barrier, inc=1, device_id=self.left, device_id_type=MESH)
+
+        peers = 1 + self.has_right.astype(jnp.int32) + self.has_left.astype(jnp.int32)
+        pl.semaphore_wait(barrier, peers)
+
+
+class Scatter:
+    def __init__(self, place, cut, part, across_a, line_a, line_b, across_b, send, recv):
+        self.at, self.cut, self.part = place, cut, part
+        self.across_a, self.line_a, self.line_b, self.across_b = across_a, line_a, line_b, across_b
+        self.send, self.recv = send, recv
+
+    @staticmethod
+    def scratch(chunks, lines, rows, width, cut):
+        return [
+            VMEM((chunks, 2, lines, rows, width), jnp.bfloat16),
+            VMEM((chunks, lines, rows, cut), jnp.bfloat16),
+            VMEM((chunks, lines + 1, rows, cut), jnp.bfloat16),
+            VMEM((chunks, lines + 1, 2, rows, width - cut), jnp.bfloat16),
+            VMEM((chunks, rows, width - cut), jnp.bfloat16),
+            pltpu.SemaphoreType.DMA((chunks, 2 * lines + 2)),
+            pltpu.SemaphoreType.DMA((chunks, 2 * lines + 4)),
+        ]
+
+    def low(self, c, j):
+        return self.part.at[c, self.at.y, j, :, : self.cut]
+
+    def high(self, c, j):
+        return self.part.at[c, :, j, :, self.cut :]
+
+    def copy_across_a(self, c):
+        return remote(
+            self.part.at[c, self.at.other, :, :, : self.cut],
+            self.across_a.at[c],
+            self.send.at[c, 0],
+            self.recv.at[c, 0],
+            self.at.across,
+        )
+
+    def copy_across_b(self, c):
+        return remote(
+            self.part.at[c, self.at.other, self.at.z, :, self.cut :],
+            self.across_b.at[c],
+            self.send.at[c, 1],
+            self.recv.at[c, 1],
+            self.at.across,
+        )
+
+    def copy_line(self, c, j, slot, device, first):
+        lines = self.at.lines
+        if first:
+            source, target, send, recv = self.low(c, j), self.line_a, 2, 2
+        else:
+            source, target, send, recv = self.high(c, j), self.line_b, 2 + lines, 3 + lines
+        return remote(
+            source, target.at[c, slot], self.send.at[c, send + j], self.recv.at[c, recv + slot], device
+        )
+
+    def to_right(self, c, j, first):
+        return self.copy_line(c, j, j + 1, self.at.right, first)
+
+    def to_left(self, c, j, first):
+        return self.copy_line(c, j, j, self.at.left, first)
+
+    def take(self, c, j, slot, first):
+        self.copy_line(c, j, slot, self.at.right, first).wait_recv()
+        view = self.low(c, j) if first else self.high(c, j)
+        came = (self.line_a if first else self.line_b)[c, slot]
+        view[...] = (view[...].astype(jnp.float32) + came.astype(jnp.float32)).astype(jnp.bfloat16)
+
+    def line_starts(self, c, first):
+        lines = self.at.lines
+
+        @pl.when(self.at.z == 0)
+        def _():
+            for j in range(lines - 1, 0, -1):
+                self.to_right(c, j, first).start()
+
+        @pl.when(self.at.z == lines - 1)
+        def _():
+            for j in range(lines - 1):
+                self.to_left(c, j, first).start()
+
+    def line_hop(self, c, step, first):
+        lines = self.at.lines
+
+        @pl.when(self.at.z == step)
+        def _():
+            for j in range(lines - 1, step, -1):
+                self.take(c, j, j + 1, first)
+                self.to_right(c, j, first).start()
+
+        @pl.when(self.at.z == lines - 1 - step)
+        def _():
+            for j in range(lines - 1 - step):
+                self.take(c, j, j, first)
+                self.to_left(c, j, first).start()
+
+    def line_end(self, c, total, first):
+        z = self.at.z
+        buffer = self.line_a if first else self.line_b
+
+        @pl.when(self.at.has_left)
+        def _():
+            self.copy_line(c, z, z + 1, self.at.right, first).wait_recv()
+            total[...] += buffer[c, z + 1].astype(jnp.float32)
+
+        @pl.when(self.at.has_right)
+        def _():
+            self.copy_line(c, z, z, self.at.right, first).wait_recv()
+            total[...] += buffer[c, z].astype(jnp.float32)
+
+    def step0(self, c):
+        self.copy_across_a(c).start()
+        self.line_starts(c, False)
+
+    def step(self, c, k, total_b):
+        lines = self.at.lines
+        if k == 1:
+            self.copy_across_a(c).wait_recv()
+            mine = self.part.at[c, self.at.y, :, :, : self.cut]
+            mine[...] = (
+                mine[...].astype(jnp.float32) + self.across_a[c].astype(jnp.float32)
+            ).astype(jnp.bfloat16)
+            self.line_starts(c, True)
+        elif k - 1 <= lines - 2:
+            self.line_hop(c, k - 1, True)
+        if k <= lines - 2:
+            self.line_hop(c, k, False)
+        elif k == lines - 1:
+            mine = self.high(c, self.at.z)
+            total_b[...] = mine[...].astype(jnp.float32)
+            self.line_end(c, total_b, False)
+            mine[...] = total_b[...].astype(jnp.bfloat16)
+            self.copy_across_b(c).start()
+
+    def finish(self, c, total):
+        y, z = self.at.y, self.at.z
+        low, high = total.at[:, : self.cut], total.at[:, self.cut :]
+        low[...] = self.low(c, z)[...].astype(jnp.float32)
+        self.line_end(c, low, True)
+        self.copy_across_b(c).wait_recv()
+        high[...] = self.part[c, y, z, :, self.cut :].astype(jnp.float32) + self.across_b[c].astype(
+            jnp.float32
+        )
+
+    def drain(self, c):
+        self.copy_across_a(c).wait_send()
+        self.copy_across_b(c).wait_send()
+        for first in (True, False):
+            for j in range(self.at.lines):
+
+                @pl.when(self.at.z != j)
+                def _(j=j, first=first):
+                    self.to_right(c, j, first).wait_send()
+
+
+class Gather:
+    def __init__(self, place, cut, own, full, local, send, recv):
+        self.at, self.cut, self.own, self.full = place, cut, own, full
+        self.local, self.send, self.recv = local, send, recv
+
+    @staticmethod
+    def scratch(chunks, lines):
+        return [
+            pltpu.SemaphoreType.DMA((chunks,)),
+            pltpu.SemaphoreType.DMA((chunks, 5 * lines + 1)),
+            pltpu.SemaphoreType.DMA((chunks, 3 * lines + 1)),
+        ]
+
+    def low(self, c, j):
+        target = self.full.at[c, self.at.y, j, :, : self.cut]
+        return target, target
+
+    def copy_low(self, c, j, way, mine):
+        lines = self.at.lines
+        target = self.full.at[c, self.at.y, j, :, : self.cut]
+        source = self.own(c).at[:, : self.cut] if mine else target
+        device = (self.at.right, self.at.left, self.at.across)[way]
+        recv = j + (lines if way == 2 else 0)
+        return remote(source, target, self.send.at[c, way * lines + j], self.recv.at[c, recv], device)
+
+    def copy_high(self, c, j, way):
+        lines = self.at.lines
+        view = self.full.at[c, :, j, :, self.cut :]
+        device = (self.at.right, self.at.left)[way]
+        return remote(
+            view, view, self.send.at[c, (3 + way) * lines + j], self.recv.at[c, 2 * lines + j], device
+        )
+
+    def copy_high_across(self, c):
+        lines = self.at.lines
+        return remote(
+            self.own(c).at[:, self.cut :],
+            self.full.at[c, self.at.y, self.at.z, :, self.cut :],
+            self.send.at[c, 5 * lines],
+            self.recv.at[c, 3 * lines],
+            self.at.across,
+        )
+
+    def copy_local(self, c):
+        return pltpu.make_async_copy(
+            self.own(c), self.full.at[c, self.at.y, self.at.z], self.local.at[c]
+        )
+
+    def step0(self, c):
+        z = self.at.z
+        if self.local is not None:
+            self.copy_local(c).start()
+
+        @pl.when(self.at.has_right)
+        def _():
+            self.copy_low(c, z, 0, True).start()
+
+        @pl.when(self.at.has_left)
+        def _():
+            self.copy_low(c, z, 1, True).start()
+
+        self.copy_high_across(c).start()
+        self.copy_low(c, z, 2, True).start()
+
+    def low_hop(self, c, k):
+        z, lines = self.at.z, self.at.lines
+
+        @pl.when(z >= k)
+        def _():
+            self.copy_low(c, z - k, 0, False).wait_recv()
+
+            @pl.when(self.at.has_right)
+            def _():
+                self.copy_low(c, z - k, 0, False).start()
+
+            self.copy_low(c, z - k, 2, False).start()
+
+        @pl.when(z + k < lines)
+        def _():
+            self.copy_low(c, z + k, 0, False).wait_recv()
+
+            @pl.when(self.at.has_left)
+            def _():
+                self.copy_low(c, z + k, 1, False).start()
+
+            self.copy_low(c, z + k, 2, False).start()
+
+    def high_hop(self, c, k):
+        z, lines = self.at.z, self.at.lines
+
+        @pl.when(z >= k)
+        def _():
+            self.copy_high(c, z - k, 0).wait_recv()
+
+            @pl.when(self.at.has_right)
+            def _():
+                self.copy_high(c, z - k, 0).start()
+
+        @pl.when(z + k < lines)
+        def _():
+            self.copy_high(c, z + k, 0).wait_recv()
+
+            @pl.when(self.at.has_left)
+            def _():
+                self.copy_high(c, z + k, 1).start()
+
+    def step(self, c, k):
+        lines, z = self.at.lines, self.at.z
+        if k == 1:
+            if self.local is not None:
+                self.copy_local(c).wait()
+            self.copy_high_across(c).wait_recv()
+
+            @pl.when(self.at.has_right)
+            def _():
+                self.copy_high(c, z, 0).start()
+
+            @pl.when(self.at.has_left)
+            def _():
+                self.copy_high(c, z, 1).start()
+
+        if k <= lines - 1:
+            self.low_hop(c, k)
+        if k > 1:
+            self.high_hop(c, k - 1)
+        if k == lines:
+            for j in range(lines):
+                target = self.full.at[c, self.at.other, j, :, : self.cut]
+                remote(
+                    target, target, self.send.at[c, 2 * lines + j], self.recv.at[c, lines + j], self.at.across
+                ).wait_recv()
+
+    def drain(self, c):
+        lines, z = self.at.lines, self.at.z
+        self.copy_high_across(c).wait_send()
+        for j in range(lines):
+
+            @pl.when(self.at.has_right & (z >= j))
+            def _(j=j):
+                self.copy_low(c, j, 0, False).wait_send()
+                self.copy_high(c, j, 0).wait_send()
+
+            @pl.when(self.at.has_left & (z <= j))
+            def _(j=j):
+                self.copy_low(c, j, 1, False).wait_send()
+                self.copy_high(c, j, 1).wait_send()
+
+            self.copy_low(c, j, 2, False).wait_send()
+
+
+def rows_sum(values):
+    return jnp.sum(values, axis=0, keepdims=True)
+
+
+def mean_last(values):
+    return jnp.mean(values, axis=-1, keepdims=True)
+
+
+def dot_nn(a, b):
+    return jnp.dot(a, b, preferred_element_type=jnp.float32)
+
+
+def dot_nt(a, b):
+    return lax.dot_general(a, b, (((1,), (1,)), ((), ())), preferred_element_type=jnp.float32)
+
+
+TILE = 256
+
+
+def middle_kernel(
+    lines, chunks, cut, chunk_rows, tokens_hbm, grad_hbm, heads_ref, wo_ref, gain_ref, bias_ref, up_ref, down_ref,
+    prob_ref, width_ref, mixed_hbm, branch_hbm, lifted_ref, squared_ref, hidden_ref, resid_ref, sums_ref,
+    x_own, g_own, g_chunk, own_mixed, own_branch, normal_ref, resid_own, inv_own, total, total_b, sem_in, *rest,
+):
+    place = Place(lines)
+    y, z, tp = place.y, place.z, place.tp
+    spot = y * lines + z
+    rows = chunk_rows // (2 * lines)
+    width = gain_ref.shape[-1]
+    units = up_ref.shape[1]
+    s1, s2, s3 = (Scatter(place, cut, *rest[7 * i : 7 * i + 7]) for i in range(3))
+    rest = rest[21:]
+    a1 = Gather(place, cut, lambda c: lifted_ref.at[c, y, z], lifted_ref, None, *rest[1:3])
+    a2 = Gather(place, cut, lambda c: own_branch.at[c], branch_hbm, *rest[3:6])
+    a3 = Gather(place, cut, lambda c: own_mixed.at[c], mixed_hbm, *rest[6:9])
+
+    get_x = pltpu.make_async_copy(tokens_hbm.at[:, spot], x_own, sem_in.at[0])
+    get_g = pltpu.make_async_copy(grad_hbm.at[:, spot], g_own, sem_in.at[1])
+    get_x.start()
+    get_g.start()
+    place.greet()
+    get_x.wait()
+    get_g.wait()
+    sums_ref[...] = jnp.zeros_like(sums_ref)
+
+    def own_rows(c):
+        return pl.ds(pl.multiple_of(c * chunk_rows + spot * rows, rows), rows)
+
+    def all_rows(c):
+        return pl.ds(pl.multiple_of(c * chunk_rows, chunk_rows), chunk_rows)
+
+    def tiled(n, body):
+        @pl.loop(0, n // TILE)
+        def _(i):
+            body(pl.ds(pl.multiple_of(i * TILE, TILE), TILE))
+
+    def put(part, c, cols, values):
+        part[c, :, :, :, cols] = values.astype(jnp.bfloat16).reshape(2, lines, rows, TILE)
+
+    def project(c):
+        heads = heads_ref[all_rows(c), :]
+
+        def one(cols):
+            put(s1.part, c, cols, dot_nn(heads, wo_ref[:, cols]))
+
+        tiled(width, one)
+        s1.step0(c)
+
+    def norm(c):
+        s1.finish(c, total)
+        residual = x_own[c].astype(jnp.float32) + total[...]
+        center = residual - mean_last(residual)
+        inv_std = lax.rsqrt(mean_last(center * center) + EPS)
+        normal = center * inv_std
+        resid_own[c] = residual
+        normal_ref[c] = normal
+        inv_own[c] = jnp.broadcast_to(inv_std, (rows, LANE))
+        lifted_ref[c, y, z] = (normal * gain_ref[...] + bias_ref[...]).astype(jnp.bfloat16)
+        a1.step0(c)
+
+    def feed(c):
+        get = pltpu.make_async_copy(grad_hbm.at[c], g_chunk, sem_in.at[2])
+        get.start()
+        lifted = lifted_ref[c].reshape(chunk_rows, width)
+        span = all_rows(c)
+        prob, limit = prob_ref[span, :], (width_ref[span, :] + 1) * (FF // 4)
+        get.wait()
+        g_chunk[...] = (g_chunk[...].astype(jnp.float32) * prob.reshape(2 * lines, rows, 1)).astype(
+            jnp.bfloat16
+        )
+
+        def units_of(cols):
+            active = jnp.maximum(dot_nn(lifted, up_ref[:, cols]), 0.0)
+            ids = tp * units + cols.start + lax.broadcasted_iota(jnp.int32, (chunk_rows, TILE), 1)
+            mask = (ids < limit).astype(jnp.float32)
+            squared_ref[span, cols] = (active * active * mask).astype(jnp.bfloat16)
+            back = dot_nt(g_chunk[...].reshape(chunk_rows, width), down_ref[cols, :])
+            hidden_ref[span, cols] = (back * mask * 2.0 * active).astype(jnp.bfloat16)
+
+        tiled(units, units_of)
+        hidden = hidden_ref[span, :]
+
+        def lift(cols):
+            put(s2.part, c, cols, dot_nt(hidden, up_ref[cols, :]))
+
+        tiled(width, lift)
+        s2.step0(c)
+        squared = squared_ref[span, :]
+
+        def out(cols):
+            put(s3.part, c, cols, dot_nn(squared, down_ref[:, cols]))
+
+        tiled(width, out)
+        s3.step0(c)
+
+    def norm_back(c):
+        s2.finish(c, total)
+        grad_lifted, normal = total[...], normal_ref[c]
+        sums_ref[0:1, :] += rows_sum(grad_lifted * normal)
+        sums_ref[1:2, :] += rows_sum(grad_lifted)
+        g = grad_lifted * gain_ref[...]
+        grad_resid = g_own[c].astype(jnp.float32) + inv_own[c][:, 0:1] * (
+            g - mean_last(g) - normal * mean_last(g * normal)
+        )
+        resid_ref[c] = grad_resid
+        own_branch[c] = grad_resid.astype(jnp.bfloat16)
+        a2.step0(c)
+
+    def mix(c):
+        s3.finish(c, total)
+        own_mixed[c] = (resid_own[c] + prob_ref[own_rows(c), :] * total[...]).astype(jnp.bfloat16)
+        a3.step0(c)
+
+    @pl.loop(0, chunks + 4 * lines)
+    def _(r):
+        def at(offset, task):
+            c = r - offset
+
+            @pl.when((c >= 0) & (c < chunks))
+            def _():
+                task(c)
+
+        for k in range(1, lines):
+            at(2 * lines + k, lambda c, k=k: s2.step(c, k, total_b))
+        for k in range(1, lines):
+            at(k, lambda c, k=k: s1.step(c, k, total_b))
+        for k in range(1, lines + 1):
+            at(lines + k, lambda c, k=k: a1.step(c, k))
+        for k in range(1, lines + 1):
+            at(3 * lines + k, lambda c, k=k: a2.step(c, k))
+        for k in range(1, lines):
+            at(2 * lines + k, lambda c, k=k: s3.step(c, k, total_b))
+        for k in range(1, lines + 1):
+            at(3 * lines + k, lambda c, k=k: a3.step(c, k))
+        at(3 * lines, norm_back)
+        at(lines, norm)
+        at(3 * lines, mix)
+        at(2 * lines, feed)
+        at(0, project)
+
+    @pl.loop(0, chunks)
+    def _(c):
+        for part in (s1, s2, s3, a1, a2, a3):
+            part.drain(c)
+
+
+def middle(tokens, grad_out, heads_out, w_out, ln_gain, ln_bias, w_up, w_down, router_prob, width_index):
+    lines = lax.axis_size("tp") // 2
+    count, width = tokens.shape
+    units = w_up.shape[1]
+    chunk_rows = CHUNK_ROWS
+    chunks, rows = count // chunk_rows, chunk_rows // (2 * lines)
+    cut = CUT
+    split = (chunks, 2 * lines, rows, width)
+    full = (chunks, 2, lines, rows, width)
+    any_space, vmem = pl.BlockSpec(memory_space=pl.ANY), pl.BlockSpec(memory_space=VMEM)
+    bf16, f32 = jnp.bfloat16, jnp.float32
+    scatter = Scatter.scratch(chunks, lines, rows, width, cut)
+    gather = Gather.scratch(chunks, lines)
+    outs = pl.pallas_call(
+        functools.partial(middle_kernel, lines, chunks, cut, chunk_rows),
+        out_shape=[
+            jax.ShapeDtypeStruct(full, bf16),
+            jax.ShapeDtypeStruct(full, bf16),
+            jax.ShapeDtypeStruct(full, bf16),
+            jax.ShapeDtypeStruct((count, units), bf16),
+            jax.ShapeDtypeStruct((count, units), bf16),
+            jax.ShapeDtypeStruct((chunks, rows, width), f32),
+            jax.ShapeDtypeStruct((2, width), f32),
+        ],
+        in_specs=[any_space, any_space] + [vmem] * 8,
+        out_specs=[any_space, any_space] + [vmem] * 5,
+        scratch_shapes=[
+            VMEM((chunks, rows, width), bf16),
+            VMEM((chunks, rows, width), bf16),
+            VMEM((2 * lines, rows, width), bf16),
+            VMEM((chunks, rows, width), bf16),
+            VMEM((chunks, rows, width), bf16),
+            VMEM((chunks, rows, width), f32),
+            VMEM((chunks, rows, width), f32),
+            VMEM((chunks, rows, LANE), f32),
+            VMEM((rows, width), f32),
+            VMEM((2, rows, width - cut), f32),
+            pltpu.SemaphoreType.DMA((3,)),
+        ]
+        + scatter * 3
+        + gather * 3,
+        compiler_params=pltpu.CompilerParams(
+            collective_id=1, has_side_effects=True, vmem_limit_bytes=VMEM_LIMIT
+        ),
+        cost_estimate=pl.CostEstimate(
+            flops=2 * count * width * (w_out.shape[0] + 4 * units), bytes_accessed=40 * 2**20, transcendentals=0
+        ),
+    )(
+        tokens.reshape(split),
+        grad_out.reshape(split),
+        heads_out,
+        w_out,
+        ln_gain[None],
+        ln_bias[None],
+        w_up,
+        w_down,
+        router_prob.reshape(count, 1),
+        width_index.reshape(count, 1),
+    )
+    mixed, branch, lifted, squared, hidden, resid, sums = outs
+    return (
+        mixed.reshape(count, width),
+        branch.reshape(count, width),
+        lifted.reshape(count, width),
+        squared,
+        hidden,
+        resid,
+        sums,
+    )
 
 
 def as_sent(array):
@@ -172,51 +754,24 @@
     heads_out = attended.astype(jnp.bfloat16).reshape(batches, rows_dev, local_heads * HD)
     router_col = router_prob[..., None]
     upstream = grad_out.astype(jnp.float32)
-    branch = lax.psum(
-        jnp.einsum("mte,ed->mtd", heads_out, w_out, preferred_element_type=jnp.float32).astype(
-            jnp.bfloat16
-        ),
-        "tp",
-    ).astype(jnp.float32)
-    residual = inputs + branch
-    center = residual - jnp.mean(residual, axis=-1, keepdims=True)
-    inv_std = lax.rsqrt(jnp.mean(center * center, axis=-1, keepdims=True) + EPS)
-    normal_ln = center * inv_std
-    lifted = (normal_ln * ln_gain + ln_bias).astype(jnp.bfloat16)
-    hidden = jnp.einsum("mtd,df->mtf", lifted, w_up, preferred_element_type=jnp.float32)
-    active = jnp.maximum(hidden, 0.0)
-    squared = (active * active * unit_mask).astype(jnp.bfloat16)
-    feed_out = lax.psum(
-        jnp.einsum("mtf,fd->mtd", squared, w_down, preferred_element_type=jnp.float32).astype(
-            jnp.bfloat16
-        ),
-        "tp",
-    ).astype(jnp.float32)
-    mixed_out = (residual + router_col * feed_out).astype(jnp.bfloat16)
-    grad_feed = (router_col * upstream).astype(jnp.bfloat16)
-    grad_down = jnp.einsum("mtf,mtd->fd", squared, grad_feed, preferred_element_type=jnp.float32)
-    grad_hidden = (
-        jnp.einsum("mtd,fd->mtf", grad_feed, w_down, preferred_element_type=jnp.float32)
-        * unit_mask
-        * 2.0
-        * active
-    ).astype(jnp.bfloat16)
-    grad_upw = jnp.einsum("mtd,mtf->df", lifted, grad_hidden, preferred_element_type=jnp.float32)
-    grad_lifted = lax.psum(
-        jnp.einsum("mtf,df->mtd", grad_hidden, w_up, preferred_element_type=jnp.float32).astype(
-            jnp.bfloat16
-        ),
-        "tp",
-    ).astype(jnp.float32)
-    ln_gain_part = jnp.sum(grad_lifted * normal_ln, axis=(0, 1))
-    ln_bias_part = jnp.sum(grad_lifted, axis=(0, 1))
-    grad_norm_ln = grad_lifted * ln_gain
-    grad_resid = upstream + inv_std * (
-        grad_norm_ln
-        - jnp.mean(grad_norm_ln, axis=-1, keepdims=True)
-        - normal_ln * jnp.mean(grad_norm_ln * normal_ln, axis=-1, keepdims=True)
-    )
-    grad_branch = grad_resid.astype(jnp.bfloat16)
+    count = batches * rows_dev
+    mixed_out, grad_branch, lifted, squared, grad_hidden, own_resid, ln_sums = middle(
+        tokens.reshape(count, features),
+        grad_out.reshape(count, features),
+        heads_out.reshape(count, -1),
+        w_out,
+        ln_gain,
+        ln_bias,
+        w_up,
+        w_down,
+        router_prob,
+        width_index,
+    )
+    mixed_out = mixed_out.reshape(tokens.shape)
+    grad_branch = grad_branch.reshape(tokens.shape)
+    grad_feed = (router_col * upstream).astype(jnp.bfloat16).reshape(count, features)
+    grad_down = jnp.einsum("tf,td->fd", squared, grad_feed, preferred_element_type=jnp.float32)
+    grad_upw = jnp.einsum("td,tf->df", lifted, grad_hidden, preferred_element_type=jnp.float32)
     grad_outw = jnp.einsum(
         "mte,mtd->ed", heads_out, grad_branch, preferred_element_type=jnp.float32
     )
@@ -285,54 +840,49 @@
         + jnp.einsum("mte,de->mtd", grad_k_pre, w_key, preferred_element_type=jnp.float32)
         + jnp.einsum("mte,de->mtd", grad_v_pre, w_value, preferred_element_type=jnp.float32)
     )
-    grad_normed = lax.psum(normed_part.astype(jnp.bfloat16), "tp").astype(jnp.float32)
-    gain_part = jnp.sum(grad_normed * scaled, axis=(0, 1))
+    ranks = lax.axis_size("tp")
+    tp = lax.axis_index("tp")
+    chunks = own_resid.shape[0]
+    split = (chunks, ranks, own_resid.shape[1], features)
+    grad_normed = lax.psum_scatter(
+        normed_part.astype(jnp.bfloat16)
+        .reshape(chunks, 2, ranks // 2, -1, features)
+        .swapaxes(1, 2)
+        .reshape(split),
+        "tp",
+        scatter_dimension=1,
+    ).astype(jnp.float32)
+
+    def own(array):
+        return lax.dynamic_index_in_dim(array.reshape(split[:-1] + (-1,)), tp % 2 * (ranks // 2) + tp // 2, 1, keepdims=False)
+
+    own_scaled = own(tokens).astype(jnp.float32) * own(inv_rms)
+    gain_part = jnp.sum(grad_normed * own_scaled, axis=(0, 1))
     grad_scaled = grad_normed * norm_gain
-    grad_input = grad_resid + inv_rms * (
-        grad_scaled - scaled * jnp.mean(grad_scaled * scaled, axis=-1, keepdims=True)
-    )
-    grad_in = grad_input.astype(jnp.bfloat16)
-    reduced = (
-        lax.psum_scatter(
-            gain_part.astype(jnp.bfloat16), "blk", scatter_dimension=0, tiled=True
-        ).astype(jnp.float32),
-        lax.psum_scatter(
-            grad_wq.astype(jnp.bfloat16), "blk", scatter_dimension=0, tiled=True
-        ).astype(jnp.float32),
-        lax.psum_scatter(
-            grad_wk.astype(jnp.bfloat16), "blk", scatter_dimension=0, tiled=True
-        ).astype(jnp.float32),
-        lax.psum_scatter(
-            grad_wv.astype(jnp.bfloat16), "blk", scatter_dimension=0, tiled=True
-        ).astype(jnp.float32),
-        lax.psum_scatter(
-            grad_outw.astype(jnp.bfloat16), "blk", scatter_dimension=1, tiled=True
-        ).astype(jnp.float32),
-        lax.psum_scatter(
-            ln_gain_part.astype(jnp.bfloat16), "blk", scatter_dimension=0, tiled=True
-        ).astype(jnp.float32),
-        lax.psum_scatter(
-            ln_bias_part.astype(jnp.bfloat16), "blk", scatter_dimension=0, tiled=True
-        ).astype(jnp.float32),
-        lax.psum_scatter(
-            grad_upw.astype(jnp.bfloat16), "blk", scatter_dimension=0, tiled=True
-        ).astype(jnp.float32),
-        lax.psum_scatter(
-            grad_down.astype(jnp.bfloat16), "blk", scatter_dimension=1, tiled=True
-        ).astype(jnp.float32),
-    )
+    grad_input = own_resid + own(inv_rms) * (
+        grad_scaled - own_scaled * jnp.mean(grad_scaled * own_scaled, axis=-1, keepdims=True)
+    )
+    grad_in = lax.all_gather(grad_input.astype(jnp.bfloat16), "tp", axis=1)
+    grad_in = grad_in.reshape(chunks, ranks // 2, 2, -1, features).swapaxes(1, 2).reshape(tokens.shape)
+    sums = lax.psum(jnp.concatenate([gain_part[None], ln_sums]), ("blk", "tp"))
+    sums = lax.dynamic_slice_in_dim(sums, lax.axis_index("blk") * (features // blocks), features // blocks, 1)
+    def share(array, dim):
+        return lax.psum_scatter(
+            array.astype(jnp.bfloat16), "blk", scatter_dimension=dim, tiled=True
+        ).astype(jnp.float32)
+
     return (
         mixed_out,
         grad_in,
-        reduced[0],
-        reduced[1],
-        reduced[2],
-        reduced[3],
-        reduced[4],
-        reduced[5],
-        reduced[6],
-        reduced[7],
-        reduced[8],
+        sums[0],
+        share(grad_wq, 0),
+        share(grad_wk, 0),
+        share(grad_wv, 0),
+        share(grad_outw, 1),
+        sums[1],
+        sums[2],
+        share(grad_upw, 0),
+        share(grad_down, 1),
     )
 
 

time: 1090 us -> 870 us (0.80)
  waiting for transfers between devices: 839 us -> 363 us
  Pallas kernels: 0 us -> 270 us
  matrix products: 113 us -> 79.2 us
  other arithmetic: 70.5 us -> 38.6 us
  blocking collectives: 11.1 us -> 40.9 us
  local copies, waits for them, and re-layouts: 26.5 us -> 49.3 us
    psum x3 -> x0, waiting for transfers between devices: 585 us -> none  [the longest x1 274 us: local(): lax.psum(jnp.einsum('mtf,fd->mtd', squared, w_down, preferred_element_typ...]
    pallas_call x0 -> x1, Pallas kernels: none -> 270 us  [middle(): pl.pallas_call(functools.partial(middle_kernel, lines, chunks, cut, chunk...]
    reduce_scatter x6 -> x7, waiting for transfers between devices: 167 us -> 238 us  [the longest x6 192 us: share(): lax.psum_scatter(array.astype(jnp.bfloat16), 'blk', scatter_dimension=dim...]
    psum x0 -> x1, blocking collectives: none -> 40.9 us  [local(): sums = lax.psum(jnp.concatenate([gain_part[None], ln_sums]), ('blk', 'tp'))]
    dot_general x7 -> x2, matrix products: 54 us -> 14.5 us  [the longest x1 8.32 us: local(): jnp.einsum('td,tf->df', lifted, grad_hidden, preferred_element_type=jnp.f...]
    all_gather x0 -> x1, waiting for transfers between devices: none -> 33.5 us  [local(): grad_in = lax.all_gather(grad_input.astype(jnp.bfloat16), 'tp', axis=1)]
    reduce_scatter x2, waiting for transfers between devices: 42.5 us -> 68.5 us  [local(): lax.psum_scatter(as_sent(key_terms), 'blk', scatter_dimension=0, tiled=True)]
    all_gather x1, waiting for transfers between devices: 24.7 us -> 0.01 us  [local(): value_piece = lax.all_gather(value_local, 'blk', axis=1, tiled=True)]
  transfers between devices with their start and end apart: 13 -> 12, of which waited for: 13 -> 11; matrix products, arithmetic and copies ran while one was open for 8% -> 11% of each run, Pallas kernels for 0% -> 0%
where the time goes in v1:
time: 870 us; the launch traced here: 860 us
  waiting for transfers between devices  363 us (42%)
  Pallas kernels  270 us (31%)
  matrix products  79.2 us (9%)
  local copies, waits for them, and re-layouts  49.3 us (6%)
  blocking collectives  40.9 us (5%)
  other arithmetic  38.6 us (4%)
  between operations  15 us (2%)
    pallas_call x1, Pallas kernels, middle(): pl.pallas_call(functools.partial(middle_kernel, lines, chunks, cut, chunk...  270 us
    reduce_scatter x6, waiting for transfers between devices, share(): lax.psum_scatter(array.astype(jnp.bfloat16), 'blk', scatter_dimension=dim...  192 us
    reduce_scatter x2, waiting for transfers between devices, local(): lax.psum_scatter(as_sent(key_terms), 'blk', scatter_dimension=0, tiled=True)  68.5 us
    reduce_scatter x1, waiting for transfers between devices, local(): lax.psum_scatter(normed_part.astype(jnp.bfloat16).reshape(chunks, 2, rank...  46.9 us
    psum x1, blocking collectives, local(): sums = lax.psum(jnp.concatenate([gain_part[None], ln_sums]), ('blk', 'tp'))  40.9 us
    all_gather x1, waiting for transfers between devices, local(): grad_in = lax.all_gather(grad_input.astype(jnp.bfloat16), 'tp', axis=1)  33.5 us
    all_gather x1, waiting for transfers between devices, local(): key_piece = lax.all_gather(key_local, 'blk', axis=1, tiled=True)  22.3 us
  transfers between devices with their start and end apart: 12, of which 11 were waited for; matrix products, arithmetic and copies ran while one was open for 11% of the time, Pallas kernels for 0%

profile of v1, /device:TPU:0, one launch (start us, length us, event | category | flops | bytes accessed | tf_op | source)
XLA Modules:
  0.0 860.5 jit_solution(13030752635260530385)
XLA Ops:
  7.3 3.2 fusion.21
  10.7 2.8 convolution_convert_fusion.3
  14.7 3.7 fusion.41
  19.6 1.4 copy.114
  21.0 3.7 fusion.45
  25.8 2.4 copy.111
  28.2 2.4 copy.112
  30.8 1.9 multiply_cosine_fusion
  33.5 3.1 subtract_convert_fusion.2
  40.2 2.3 pad_maximum_fusion
  42.5 22.3 %all-gather.5.cloned.1.call-done = bf16[4,1024,2,128]{3,1,2,0:T(8,128)(2,1)} async-done(((bf16[4,256,2,128]{3,1,2,0:T(8,128)(2,1)}), bf16[4,1024,2,128]{3,1,2,0:T(8,128)(2,1)}) %all-gather.5.cloned.1.call-update) | async-done | bytes 2097168 | tf_op jit(solution)/shard_map/all_gather | solution.py:727
  64.8 11.0 %conditional.2 = (f32[4,2,256]{2,1,0:T(2,128)S(1)}, f32[4,2,256]{2,1,0:T(2,128)S(1)}, f32[4,2,256]{2,1,0:T(2,128)S(1)}, f32[4,2,256,128]{2,3,1,0:T(8,128)S(1)}) conditional(s32[]{:T(128)} %convert_element_type.152, (s32[1024]{0:T(1024)S(1)}, s32[256]{0:T(256)S(1)}, s32[1024]{0:T(1024)S(1)}, s32[4,256]{1,0:T(4,128)S(1)}, ...), branch_computations={%region_3.6_spmd, %region_6.7_spmd} | conditional | flops 1103362048 | bytes 44119100 | solution.py:749
  65.8 3.8 fusion.2
  69.7 3.0 fusion.5
  72.7 3.1 fusion.4
  77.3 270.1 %shard_map.230 = (bf16[8,2,4,16,2048]{4,3,2,1,0:T(8,128)(2,1)}, bf16[8,2,4,16,2048]{4,3,2,1,0:T(8,128)(2,1)}, bf16[8,2,4,16,2048]{4,3,2,1,0:T(8,128)(2,1)}, bf16...) custom-call(bf16[8,8,16,2048]{3,2,1,0:T(8,128)(2,1)} %bitcast.163, ...), custom_call_target="tpu_custom_call" | custom-call | flops 18253611008 | bytes 41943040 | tf_op jit(solution)/shard_map/pallas_call | solution.py:540
  347.4 3.8 convolution_convert_fusion.2
  351.8 32.8 %while.18 = (s32[]{:T(128)}, f32[4,256,2,128]{3,1,2,0:T(8,128)S(1)}, bf16[4,4,256,2,128]{4,2,3,1,0:T(8,128)(2,1)}, bf16[4,4,256,2,128]{2,4,3,1,0:T(8,128)(2,1)},...) while((s32[]{:T(128)}, ...), condition=%wide.region_11.12_spmd.clone, body=%wide.region_8.11_spmd.clone.sunk | while | flops 676135424 | bytes 24277424 | solution.py:818
  353.1 7.6 conditional.5
  353.5 1.9 bitcast_select_fusion
  355.3 1.5 fusion.12
  357.3 1.8 fusion.13
  359.1 1.5 convolution_bitcast_fusion.1
  361.6 1.2 copy.145
  363.7 1.9 constant_dynamic-update-slice_fusion.4
  368.0 1.2 copy.145
  370.0 1.9 constant_dynamic-update-slice_fusion.4
  374.3 1.2 copy.145
  376.4 1.9 constant_dynamic-update-slice_fusion.4
  380.7 1.2 copy.145
  382.8 1.9 constant_dynamic-update-slice_fusion.4
  385.3 45.3 %reduce-scatter.10.cloned.1.call-done = bf16[1,4,256,2,128]{4,2,3,1,0:T(8,128)(2,1)} async-done(((bf16[4,4,256,2,128]{4,2,3,1,0:T(8,128)(2,1)}), bf16[1,4,256,2,128]{4,2,3,1,0:T(8,128)(2,1)}) %reduce-scatter.10.cloned.1.call-update) | async-done | bytes 524304 | tf_op jit(solution)/shard_map/reduce_scatter | solution.py:823
  432.6 4.6 fusion.43
  437.3 4.8 fusion.39
  442.0 23.2 %reduce-scatter.12.cloned.1.call-done = bf16[1,4,256,2,128]{2,4,3,1,0:T(8,128)(2,1)} async-done(((bf16[4,4,256,2,128]{2,4,3,1,0:T(8,128)(2,1)}), bf16[1,4,256,2,128]{2,4,3,1,0:T(8,128)(2,1)}) %reduce-scatter.12.cloned.1.call-update) | async-done | bytes 524304 | tf_op jit(solution)/shard_map/reduce_scatter | solution.py:823
  465.2 7.2 add_convert_fusion
  472.4 2.5 copy.89
  476.0 4.5 fusion.27
  480.6 5.5 fusion.25
  486.3 5.2 fusion.24
  491.5 4.9 fusion.26
  496.7 3.1 multiply_convert_fusion
  499.8 6.2 convolution_convert_fusion
  506.1 1.5 copy-done.32
  507.6 8.3 convolution_convert_fusion.1
  516.1 46.9 %reduce-scatter.14.cloned.1.call-done = bf16[8,1,16,2048]{3,2,0,1:T(8,128)(2,1)} async-done(((bf16[8,8,16,2048]{3,2,0,1:T(8,128)(2,1)}), bf16[8,1,16,2048]{3,2,0,1:T(8,128)(2,1)}) %reduce-scatter.14.cloned.1.call-update) | async-done | bytes 524304 | tf_op jit(solution)/shard_map/reduce_scatter | solution.py:847
  563.1 1.6 fusion.34
  564.7 2.4 fusion.33
  567.2 23.1 %reduce-scatter.22.cloned.1.call-done = bf16[256,512]{1,0:T(8,128)(2,1)} async-done(((bf16[256,2048]{1,0:T(8,128)(2,1)}), bf16[256,512]{1,0:T(8,128)(2,1)}) %reduce-scatter.22.cloned.1.call-update) | async-done | bytes 262160 | tf_op jit(solution)/shard_map/reduce_scatter | solution.py:870
  590.3 1.8 convert_element_type.181
  592.1 26.2 %reduce-scatter.18.cloned.1.call-done = bf16[512,256]{1,0:T(8,128)(2,1)} async-done(((bf16[2048,256]{1,0:T(8,128)(2,1)}), bf16[512,256]{1,0:T(8,128)(2,1)}) %reduce-scatter.18.cloned.1.call-update) | async-done | bytes 262160 | tf_op jit(solution)/shard_map/reduce_scatter | solution.py:870
  618.3 1.8 convert_element_type.177
  620.1 26.4 %reduce-scatter.16.cloned.1.call-done = bf16[512,256]{1,0:T(8,128)(2,1)} async-done(((bf16[2048,256]{1,0:T(8,128)(2,1)}), bf16[512,256]{1,0:T(8,128)(2,1)}) %reduce-scatter.16.cloned.1.call-update) | async-done | bytes 262160 | tf_op jit(solution)/shard_map/reduce_scatter | solution.py:870
  646.5 1.8 convert_element_type.175
  648.2 25.7 %reduce-scatter.20.cloned.1.call-done = bf16[512,256]{1,0:T(8,128)(2,1)} async-done(((bf16[2048,256]{1,0:T(8,128)(2,1)}), bf16[512,256]{1,0:T(8,128)(2,1)}) %reduce-scatter.20.cloned.1.call-update) | async-done | bytes 262160 | tf_op jit(solution)/shard_map/reduce_scatter | solution.py:870
  673.9 1.8 convert_element_type.179
  675.7 45.3 %reduce-scatter.26.cloned.1.call-done = bf16[1024,512]{1,0:T(8,128)(2,1)} async-done(((bf16[1024,2048]{1,0:T(8,128)(2,1)}), bf16[1024,512]{1,0:T(8,128)(2,1)}) %reduce-scatter.26.cloned.1.call-update) | async-done | bytes 1048592 | tf_op jit(solution)/shard_map/reduce_scatter | solution.py:870
  721.0 2.8 convert_element_type.187
  723.8 44.8 %reduce-scatter.24.cloned.1.call-done = bf16[512,1024]{1,0:T(8,128)(2,1)} async-done(((bf16[2048,1024]{1,0:T(8,128)(2,1)}), bf16[512,1024]{1,0:T(8,128)(2,1)}) %reduce-scatter.24.cloned.1.call-update) | async-done | bytes 1048592 | tf_op jit(solution)/shard_map/reduce_scatter | solution.py:870
  768.6 2.8 convert_element_type.183
  771.4 40.9 %psum.7 = f32[3,2048]{1,0:T(4,128)S(1)} all-reduce(f32[3,2048]{1,0:T(4,128)S(1)} %pad_maximum_fusion.2), channel_id=1, replica_groups=mesh['blk'=4,'tp'=8] {'blk','tp'}, use_global_device_ids=true, to_apply=%region_17.18 | all-reduce | flops 6144 | bytes 49152 | tf_op jit(solution)/shard_map/psum | solution.py:867
  813.0 33.5 %all-gather.9.cloned.1.call-done = bf16[8,128,2048]{2,1,0:T(8,128)(2,1)} async-done(((bf16[8,16,2048]{2,1,0:T(8,128)(2,1)}), bf16[8,128,2048]{2,1,0:T(8,128)(2,1)}) %all-gather.9.cloned.1.call-update) | async-done | bytes 4194320 | tf_op jit(solution)/shard_map/all_gather | solution.py:865
  846.5 4.9 copy.90
  851.4 2.0 copy.175
  (166 shorter events, 27.5 us)
Async XLA Ops:
  7.2 13.8 %copy-start = (bf16[2048,256]{1,0:T(8,128)(2,1)S(1)}, bf16[2048,256]{1,0:T(8,128)(2,1)}, u32[]{:S(2)}) copy-start(bf16[2048,256]{1,0:T(8,128)(2,1)} %param.27) | copy-start | bytes 3145732
  7.2 3.3 copy-start.25
  7.2 35.3 %all-gather.7.cloned.1.call-start = ((), (), s32[]{:S(2)}) async-start(), calls=%async_computation.10 | async-start | bytes 2621440 | tf_op jit(solution)/shard_map/all_gather | solution.py:728
  7.2 3.5 copy-start.3
  10.7 3.9 copy-start.20
  14.6 50.2 %all-gather.5.cloned.1.call-start = ((), (), s32[]{:S(2)}) async-start(), calls=%async_computation.9 | async-start | bytes 2621440 | tf_op jit(solution)/shard_map/all_gather | solution.py:727
  24.8 5.8 copy-start.28
  32.7 0.8 copy-start.4
  32.7 3.9 copy-start.6
  33.5 4.5 copy-start.29
  33.5 4.5 copy-start.26
  36.7 5.8 copy-start.30
  37.8 392.9 %reduce-scatter.10.cloned.1.call-start = ((), (), s32[]{:S(2)}) async-start(), calls=%async_computation.11 | async-start | bytes 2621440 | tf_op jit(solution)/shard_map/reduce_scatter | solution.py:823
  65.8 3.9 copy-start.9
  76.0 271.4 %copy-start.18 = (bf16[4,256,2,128]{1,3,2,0:T(8,128)(2,1)}, bf16[4,256,2,128]{1,3,2,0:T(8,128)(2,1)S(1)}, u32[]{:S(2)}) copy-start(bf16[4,256,2,128]{1,3,2,0:T(8,128)(2,1)S(1)} %fusion.55) | copy-start | bytes 1572868
  360.6 0.8 copy-start.1
  360.6 1.0 copy-start.2
  367.0 0.8 copy-start.1
  367.0 1.0 copy-start.2
  373.3 0.8 copy-start.1
  373.4 1.0 copy-start.2
  379.7 0.8 copy-start.1
  379.7 1.0 copy-start.2
  384.6 47.1 %copy-start.5 = (f32[4,256,64]{2,1,0:T(8,128)S(1)}, f32[4,256,64]{2,1,0:T(8,128)}, u32[]{:S(2)}) copy-start(f32[4,256,64]{2,1,0:T(8,128)} %copy-done.4) | copy-start | bytes 786436
  384.6 47.1 %copy-start.7 = (f32[4,256,64]{2,1,0:T(8,128)S(1)}, f32[4,256,64]{2,1,0:T(8,128)}, u32[]{:S(2)}) copy-start(f32[4,256,64]{2,1,0:T(8,128)} %copy-done.6) | copy-start | bytes 786436
  384.7 80.6 %reduce-scatter.12.cloned.1.call-start = ((), (), s32[]{:S(2)}) async-start(), calls=%async_computation.12 | async-start | bytes 2621440 | tf_op jit(solution)/shard_map/reduce_scatter | solution.py:823
  385.2 177.8 %reduce-scatter.14.cloned.1.call-start = ((), (), s32[]{:S(2)}) async-start(), calls=%async_computation.13 | async-start | bytes 4718592 | tf_op jit(solution)/shard_map/reduce_scatter | solution.py:847
  432.6 4.7 copy-start.10
  432.6 4.6 copy-start.12
  432.6 4.6 copy-start.14
  432.6 4.6 copy-start.16
  432.6 4.6 copy-start.21
  437.2 28.0 %copy-start.22 = (bf16[2048,256]{1,0:T(8,128)(2,1)S(1)}, bf16[2048,256]{1,0:T(8,128)(2,1)}, u32[]{:S(2)}) copy-start(bf16[2048,256]{1,0:T(8,128)(2,1)} %param.29) | copy-start | bytes 3145732
  475.0 1.0 copy-start.19
  475.0 5.6 copy-start.15
  475.0 5.6 copy-start.17
  475.0 115.2 %reduce-scatter.22.cloned.1.call-start = ((), (), s32[]{:S(2)}) async-start(), calls=%async_computation.17 | async-start | bytes 1310720 | tf_op jit(solution)/shard_map/reduce_scatter | solution.py:870
  480.5 5.7 copy-start.11
  480.5 5.7 copy-start.13
  480.6 137.7 %reduce-scatter.18.cloned.1.call-start = ((), (), s32[]{:S(2)}) async-start(), calls=%async_computation.15 | async-start | bytes 1310720 | tf_op jit(solution)/shard_map/reduce_scatter | solution.py:870
  486.2 5.3 copy-start.24
  486.2 160.3 %reduce-scatter.16.cloned.1.call-start = ((), (), s32[]{:S(2)}) async-start(), calls=%async_computation.14 | async-start | bytes 1310720 | tf_op jit(solution)/shard_map/reduce_scatter | solution.py:870
  491.4 182.5 %reduce-scatter.20.cloned.1.call-start = ((), (), s32[]{:S(2)}) async-start(), calls=%async_computation.16 | async-start | bytes 1310720 | tf_op jit(solution)/shard_map/reduce_scatter | solution.py:870
  496.4 3.4 copy-start.31
  496.4 224.6 %reduce-scatter.26.cloned.1.call-start = ((), (), s32[]{:S(2)}) async-start(), calls=%async_computation.19 | async-start | bytes 5242880 | tf_op jit(solution)/shard_map/reduce_scatter | solution.py:870
  506.0 1.6 copy-start.32
  506.1 262.6 %reduce-scatter.24.cloned.1.call-start = ((), (), s32[]{:S(2)}) async-start(), calls=%async_computation.18 | async-start | bytes 5242880 | tf_op jit(solution)/shard_map/reduce_scatter | solution.py:870
  516.0 48.8 %copy-start.23 = (f32[8,16,2048]{2,1,0:T(8,128)S(1)}, f32[8,16,2048]{2,1,0:T(8,128)}, u32[]{:S(2)}) copy-start(f32[8,16,2048]{2,1,0:T(8,128)} %get-tuple-element.255) | copy-start | bytes 3145732
  516.0 330.5 %all-gather.9.cloned.1.call-start = ((), (), s32[]{:S(2)}) async-start(), calls=%async_computation.20 | async-start | bytes 4718592 | tf_op jit(solution)/shard_map/all_gather | solution.py:865
  592.1 179.3 %copy-start.27 = (f32[2,2048]{1,0:T(2,128)S(1)}, f32[2,2048]{1,0:T(2,128)}, u32[]{:S(2)}) copy-start(f32[2,2048]{1,0:T(2,128)} %get-tuple-element.262) | copy-start | bytes 49156
  846.5 4.9 copy-start.8
Sparse Core Ops, SparseCore 0:
  14.7 25.2 all-gather.6
  42.2 22.5 all-gather.4
  384.8 45.8 reduce-scatter.9
  433.7 31.4 reduce-scatter.11
  475.1 87.8 reduce-scatter.13
  565.6 24.6 reduce-scatter.21
  593.4 24.8 reduce-scatter.17
  621.6 24.8 reduce-scatter.15
  649.0 24.8 reduce-scatter.19
  676.5 44.4 reduce-scatter.25
  724.1 44.4 reduce-scatter.23
  771.5 74.9 all-gather.8

commit v2 on v1

--- a/solution.py
+++ b/solution.py
@@ -17,6 +17,7 @@
 CHUNK_ROWS = 128
 CUT = 1280
 VMEM_LIMIT = 60 * 2**20
+RING = 4
 
 
 MESH = pl.DeviceIdType.MESH
@@ -41,20 +42,23 @@
         self.left = (blk, jnp.maximum(self.z - 1, 0) * 2 + self.y)
         self.has_right, self.has_left = self.z < lines - 1, self.z > 0
 
-    def greet(self):
-        barrier = pltpu.get_barrier_semaphore()
-        pl.semaphore_signal(barrier, inc=1, device_id=self.across, device_id_type=MESH)
-
-        @pl.when(self.has_right)
-        def _():
-            pl.semaphore_signal(barrier, inc=1, device_id=self.right, device_id_type=MESH)
-
-        @pl.when(self.has_left)
-        def _():
-            pl.semaphore_signal(barrier, inc=1, device_id=self.left, device_id_type=MESH)
-
-        peers = 1 + self.has_right.astype(jnp.int32) + self.has_left.astype(jnp.int32)
-        pl.semaphore_wait(barrier, peers)
+
+def greet(*axes):
+    place = {axis: lax.axis_index(axis) for axis in ("blk", "tp")}
+    peers = 0
+    for axis in axes:
+        size = lax.axis_size(axis)
+        for k in range(1, size):
+            peer = dict(place)
+            peer[axis] = (place[axis] + k) % size
+            pl.semaphore_signal(
+                pltpu.get_barrier_semaphore(),
+                inc=1,
+                device_id=(peer["blk"], peer["tp"]),
+                device_id_type=MESH,
+            )
+        peers += size - 1
+    pl.semaphore_wait(pltpu.get_barrier_semaphore(), peers)
 
 
 class Scatter:
@@ -71,6 +75,11 @@
             VMEM((chunks, lines + 1, rows, cut), jnp.bfloat16),
             VMEM((chunks, lines + 1, 2, rows, width - cut), jnp.bfloat16),
             VMEM((chunks, rows, width - cut), jnp.bfloat16),
+        ]
+
+    @staticmethod
+    def semaphores(chunks, lines):
+        return [
             pltpu.SemaphoreType.DMA((chunks, 2 * lines + 2)),
             pltpu.SemaphoreType.DMA((chunks, 2 * lines + 4)),
         ]
@@ -358,6 +367,98 @@
             self.copy_low(c, j, 2, False).wait_send()
 
 
+class BlockScatter:
+    def __init__(self, blocks, slice_of, part, from_core, from_chip, send, recv):
+        self.blk, self.tp = lax.axis_index("blk"), lax.axis_index("tp")
+        self.chips, self.chip, self.core = blocks // 2, self.blk // 2, self.blk % 2
+        self.slice_of, self.part = slice_of, part
+        self.from_core, self.from_chip, self.send, self.recv = from_core, from_chip, send, recv
+
+    @staticmethod
+    def scratch(blocks, shape):
+        chips = blocks // 2
+        return [
+            VMEM((blocks,) + shape, jnp.bfloat16),
+            VMEM((chips,) + shape, jnp.bfloat16),
+            VMEM((max(chips - 1, 1),) + shape, jnp.bfloat16),
+            pltpu.SemaphoreType.DMA((2, chips)),
+            pltpu.SemaphoreType.DMA((2, chips)),
+        ]
+
+    def to_core(self, k):
+        return remote(
+            self.part.at[k * 2 + 1 - self.core],
+            self.from_core.at[k],
+            self.send.at[0, k],
+            self.recv.at[0, k],
+            (self.chip * 2 + 1 - self.core, self.tp),
+        )
+
+    def to_chip(self, k):
+        return remote(
+            self.part.at[k * 2 + self.core],
+            self.from_chip.at[(self.chip - k + self.chips) % self.chips - 1],
+            self.send.at[1, k],
+            self.recv.at[1, (self.chip - k + self.chips) % self.chips],
+            (k * 2 + self.core, self.tp),
+        )
+
+    def came_chip(self, i):
+        k = (self.chip + i) % self.chips
+        return remote(
+            self.part.at[k * 2 + self.core],
+            self.from_chip.at[i - 1],
+            self.send.at[1, k],
+            self.recv.at[1, i],
+            (k * 2 + self.core, self.tp),
+        )
+
+    def all_first(self):
+        @pl.loop(0, self.chips)
+        def _(i):
+            self.first(i)
+
+    def all_second(self):
+        @pl.loop(0, self.chips)
+        def _(i):
+            self.second(i)
+
+    def first(self, i):
+        k = (self.chip + 1 + i) % self.chips
+        self.slice_of(k * 2 + 1 - self.core, self.part.at[k * 2 + 1 - self.core])
+        self.to_core(k).start()
+
+    def second(self, i):
+        k = (self.chip + 1 + i) % self.chips
+        mine = self.part.at[k * 2 + self.core]
+        self.slice_of(k * 2 + self.core, mine)
+        self.to_core(k).wait_recv()
+        mine[...] = (mine[...].astype(jnp.float32) + self.from_core[k].astype(jnp.float32)).astype(
+            jnp.bfloat16
+        )
+
+        @pl.when(k != self.chip)
+        def _():
+            self.to_chip(k).start()
+
+    def third(self, out):
+        out[...] = self.part[self.blk].astype(jnp.float32)
+
+        @pl.loop(1, self.chips)
+        def _(i):
+            self.came_chip(i).wait_recv()
+            out[...] += self.from_chip[i - 1].astype(jnp.float32)
+
+    def drain(self):
+        @pl.loop(0, self.chips)
+        def _(k):
+            self.to_core(k).wait_send()
+
+            @pl.when(k != self.chip)
+            def _():
+                self.to_chip(k).wait_send()
+
+
 def rows_sum(values):
     return jnp.sum(values, axis=0, keepdims=True)
 
@@ -374,13 +475,18 @@
     return lax.dot_general(a, b, (((1,), (1,)), ((), ())), preferred_element_type=jnp.float32)
 
 
+def dot_tn(a, b):
+    return lax.dot_general(a, b, (((0,), (0,)), ((), ())), preferred_element_type=jnp.float32)
+
+
 TILE = 256
 
 
 def middle_kernel(
     lines, chunks, cut, chunk_rows, tokens_hbm, grad_hbm, heads_ref, wo_ref, gain_ref, bias_ref, up_ref, down_ref,
-    prob_ref, width_ref, mixed_hbm, branch_hbm, lifted_ref, squared_ref, hidden_ref, resid_ref, sums_ref,
-    x_own, g_own, g_chunk, own_mixed, own_branch, normal_ref, resid_own, inv_own, total, total_b, sem_in, *rest,
+    prob_ref, width_ref, branch_hbm, feed_hbm, input_ref, resid_ref, sums_ref, grad_up_ref, grad_down_ref,
+    x_own, g_own, g_all, own_branch, feed_part, lifted_ref, squared_ref, hidden_ref, normal_ref, inv_own, total,
+    total_b, sem_in, sem_g, sem_feed, *rest,
 ):
     place = Place(lines)
     y, z, tp = place.y, place.z, place.tp
@@ -388,17 +494,51 @@
     rows = chunk_rows // (2 * lines)
     width = gain_ref.shape[-1]
     units = up_ref.shape[1]
-    s1, s2, s3 = (Scatter(place, cut, *rest[7 * i : 7 * i + 7]) for i in range(3))
-    rest = rest[21:]
-    a1 = Gather(place, cut, lambda c: lifted_ref.at[c, y, z], lifted_ref, None, *rest[1:3])
-    a2 = Gather(place, cut, lambda c: own_branch.at[c], branch_hbm, *rest[3:6])
-    a3 = Gather(place, cut, lambda c: own_mixed.at[c], mixed_hbm, *rest[6:9])
+    blocks = lax.axis_size("blk")
+    s1, s2 = Scatter(place, cut, *rest[:5], *rest[5:7]), Scatter(place, cut, *rest[:5], *rest[7:9])
+    a1 = Gather(place, cut, lambda c: lifted_ref.at[c, y, z], lifted_ref, None, *rest[10:12])
+    a2 = Gather(place, cut, lambda c: own_branch.at[c], branch_hbm, *rest[12:15])
+    share = width // blocks
+
+    def up_slice(target, out):
+        step = min(TILE, share)
+
+        @pl.loop(0, share // step)
+        def _(i):
+            lanes = pl.ds(pl.multiple_of(target * share + i * step, step), step)
+            lifted = lifted_ref[:, :, :, :, lanes].reshape(chunks * chunk_rows, step)
+            out[pl.ds(pl.multiple_of(i * step, step), step), :] = dot_tn(lifted, hidden_ref[...]).astype(
+                jnp.bfloat16
+            )
+
+    def down_slice(target, out):
+        lanes = pl.ds(pl.multiple_of(target * share, share), share)
+
+        @pl.loop(0, units // TILE)
+        def _(i):
+            cols = pl.ds(pl.multiple_of(i * TILE, TILE), TILE)
+            grad = g_all[:, :, :, lanes].reshape(chunks * chunk_rows, share)
+            out[cols, :] = dot_tn(squared_ref[:, cols], grad).astype(jnp.bfloat16)
+
+    grad_up = BlockScatter(blocks, up_slice, *rest[15:20])
+    grad_down = BlockScatter(blocks, down_slice, *rest[20:25])
 
     get_x = pltpu.make_async_copy(tokens_hbm.at[:, spot], x_own, sem_in.at[0])
     get_g = pltpu.make_async_copy(grad_hbm.at[:, spot], g_own, sem_in.at[1])
     get_x.start()
     get_g.start()
-    place.greet()
+
+    def get_grad(c):
+        return pltpu.make_async_copy(grad_hbm.at[c], g_all.at[c], sem_g.at[c])
+
+    def put_feed(c):
+        return pltpu.make_async_copy(feed_part.at[c % 2], feed_hbm.at[c], sem_feed.at[c])
+
+    @pl.loop(0, chunks)
+    def _(c):
+        get_grad(c).start()
+
+    greet("tp", "blk")
     get_x.wait()
     get_g.wait()
     sums_ref[...] = jnp.zeros_like(sums_ref)
@@ -432,29 +572,26 @@
         center = residual - mean_last(residual)
         inv_std = lax.rsqrt(mean_last(center * center) + EPS)
         normal = center * inv_std
-        resid_own[c] = residual
+        input_ref[c] = residual
         normal_ref[c] = normal
         inv_own[c] = jnp.broadcast_to(inv_std, (rows, LANE))
         lifted_ref[c, y, z] = (normal * gain_ref[...] + bias_ref[...]).astype(jnp.bfloat16)
         a1.step0(c)
 
     def feed(c):
-        get = pltpu.make_async_copy(grad_hbm.at[c], g_chunk, sem_in.at[2])
-        get.start()
+        s1.drain(c)
         lifted = lifted_ref[c].reshape(chunk_rows, width)
         span = all_rows(c)
         prob, limit = prob_ref[span, :], (width_ref[span, :] + 1) * (FF // 4)
-        get.wait()
-        g_chunk[...] = (g_chunk[...].astype(jnp.float32) * prob.reshape(2 * lines, rows, 1)).astype(
-            jnp.bfloat16
-        )
+        get_grad(c).wait()
+        g_all[c] = (g_all[c].astype(jnp.float32) * prob.reshape(2 * lines, rows, 1)).astype(jnp.bfloat16)
 
         def units_of(cols):
             active = jnp.maximum(dot_nn(lifted, up_ref[:, cols]), 0.0)
             ids = tp * units + cols.start + lax.broadcasted_iota(jnp.int32, (chunk_rows, TILE), 1)
             mask = (ids < limit).astype(jnp.float32)
             squared_ref[span, cols] = (active * active * mask).astype(jnp.bfloat16)
-            back = dot_nt(g_chunk[...].reshape(chunk_rows, width), down_ref[cols, :])
+            back = dot_nt(g_all[c].reshape(chunk_rows, width), down_ref[cols, :])
             hidden_ref[span, cols] = (back * mask * 2.0 * active).astype(jnp.bfloat16)
 
         tiled(units, units_of)
@@ -467,11 +604,15 @@
         s2.step0(c)
         squared = squared_ref[span, :]
 
+        @pl.when(c >= 2)
+        def _():
+            put_feed(c - 2).wait()
+
         def out(cols):
-            put(s3.part, c, cols, dot_nn(squared, down_ref[:, cols]))
+            put(feed_part, c % 2, cols, dot_nn(squared, down_ref[:, cols]))
 
         tiled(width, out)
-        s3.step0(c)
+        put_feed(c).start()
 
     def norm_back(c):
         s2.finish(c, total)
@@ -486,11 +627,6 @@
         own_branch[c] = grad_resid.astype(jnp.bfloat16)
         a2.step0(c)
 
-    def mix(c):
-        s3.finish(c, total)
-        own_mixed[c] = (resid_own[c] + prob_ref[own_rows(c), :] * total[...]).astype(jnp.bfloat16)
-        a3.step0(c)
-
     @pl.loop(0, chunks + 4 * lines)
     def _(r):
         def at(offset, task):
@@ -508,20 +644,25 @@
             at(lines + k, lambda c, k=k: a1.step(c, k))
         for k in range(1, lines + 1):
             at(3 * lines + k, lambda c, k=k: a2.step(c, k))
-        for k in range(1, lines):
-            at(2 * lines + k, lambda c, k=k: s3.step(c, k, total_b))
-        for k in range(1, lines + 1):
-            at(3 * lines + k, lambda c, k=k: a3.step(c, k))
         at(3 * lines, norm_back)
         at(lines, norm)
-        at(3 * lines, mix)
         at(2 * lines, feed)
         at(0, project)
+        for k, task in enumerate((grad_up.all_first, grad_down.all_first, grad_up.all_second, grad_down.all_second)):
+            pl.when(r == chunks + 2 * lines + k)(task)
+
+    grad_up.third(grad_up_ref)
+    grad_down.third(grad_down_ref)
+    for c in range(max(chunks - 2, 0), chunks):
+        put_feed(c).wait()
 
     @pl.loop(0, chunks)
     def _(c):
-        for part in (s1, s2, s3, a1, a2, a3):
+        for part in (s2, a1, a2):
             part.drain(c)
+
+    grad_up.drain()
+    grad_down.drain()
 
 
 def middle(tokens, grad_out, heads_out, w_out, ln_gain, ln_bias, w_up, w_down, router_prob, width_index):
@@ -535,41 +676,49 @@
     full = (chunks, 2, lines, rows, width)
     any_space, vmem = pl.BlockSpec(memory_space=pl.ANY), pl.BlockSpec(memory_space=VMEM)
     bf16, f32 = jnp.bfloat16, jnp.float32
-    scatter = Scatter.scratch(chunks, lines, rows, width, cut)
-    gather = Gather.scratch(chunks, lines)
+    dma = pltpu.SemaphoreType.DMA
+    blocks = lax.axis_size("blk")
+    share = width // blocks
     outs = pl.pallas_call(
         functools.partial(middle_kernel, lines, chunks, cut, chunk_rows),
         out_shape=[
             jax.ShapeDtypeStruct(full, bf16),
             jax.ShapeDtypeStruct(full, bf16),
-            jax.ShapeDtypeStruct(full, bf16),
-            jax.ShapeDtypeStruct((count, units), bf16),
-            jax.ShapeDtypeStruct((count, units), bf16),
+            jax.ShapeDtypeStruct((chunks, rows, width), f32),
             jax.ShapeDtypeStruct((chunks, rows, width), f32),
             jax.ShapeDtypeStruct((2, width), f32),
+            jax.ShapeDtypeStruct((share, units), f32),
+            jax.ShapeDtypeStruct((units, share), f32),
         ],
         in_specs=[any_space, any_space] + [vmem] * 8,
         out_specs=[any_space, any_space] + [vmem] * 5,
         scratch_shapes=[
             VMEM((chunks, rows, width), bf16),
             VMEM((chunks, rows, width), bf16),
-            VMEM((2 * lines, rows, width), bf16),
+            VMEM(split, bf16),
             VMEM((chunks, rows, width), bf16),
-            VMEM((chunks, rows, width), bf16),
-            VMEM((chunks, rows, width), f32),
+            VMEM((2,) + full[1:], bf16),
+            VMEM(full, bf16),
+            VMEM((count, units), bf16),
+            VMEM((count, units), bf16),
             VMEM((chunks, rows, width), f32),
             VMEM((chunks, rows, LANE), f32),
             VMEM((rows, width), f32),
             VMEM((2, rows, width - cut), f32),
-            pltpu.SemaphoreType.DMA((3,)),
+            dma((2,)),
+            dma((chunks,)),
+            dma((chunks,)),
         ]
-        + scatter * 3
-        + gather * 3,
+        + Scatter.scratch(chunks, lines, rows, width, cut)
+        + Scatter.semaphores(chunks, lines) * 2
+        + Gather.scratch(chunks, lines) * 2
+        + BlockScatter.scratch(blocks, (share, units))
+        + BlockScatter.scratch(blocks, (units, share)),
         compiler_params=pltpu.CompilerParams(
             collective_id=1, has_side_effects=True, vmem_limit_bytes=VMEM_LIMIT
         ),
         cost_estimate=pl.CostEstimate(
-            flops=2 * count * width * (w_out.shape[0] + 4 * units), bytes_accessed=40 * 2**20, transcendentals=0
+            flops=2 * count * width * (w_out.shape[0] + 6 * units), bytes_accessed=40 * 2**20, transcendentals=0
         ),
     )(
         tokens.reshape(split),
@@ -583,20 +732,369 @@
         router_prob.reshape(count, 1),
         width_index.reshape(count, 1),
     )
-    mixed, branch, lifted, squared, hidden, resid, sums = outs
-    return (
-        mixed.reshape(count, width),
-        branch.reshape(count, width),
-        lifted.reshape(count, width),
-        squared,
-        hidden,
-        resid,
-        sums,
+    return (outs[0].reshape(count, width),) + tuple(outs[1:])
+
+
+def turn_back(grad, cos_rows, sin_rows):
+    return grad * cos_rows - pltpu.roll(grad, HD // 2, 1) * sin_rows
+
+
+def back_kernel(
+    lines, blocks, batches, chunks, cut, chunk_rows, tokens_hbm, keys_hbm, values_hbm, feed_hbm, input_ref,
+    resid_ref, branch_ref, query_ref, heads_ref, normed_ref, wq_ref, wk_ref, wv_ref, wo_ref, gain_ref, lse_ref,
+    begin_ref, count_ref, prob_ref, cos_ref, sin_ref, sums_ref, mixed_hbm, in_hbm, gq_ref, gk_ref, gv_ref, go_ref,
+    small_ref, x_own, own_in, own_mixed, key_mb, value_mb, grad_mb, delta_mb, dq_mb, stage, own, came, pre, total, total_b,
+    grad_w, small, small_blk, small_part, small_tp, sem_in, sem_feed, sem_kv, sem_send, sem_recv, sem_free, sem_blk, sem_tp,
+    *rest,
+):
+    place = Place(lines)
+    blk, tp, y, z = lax.axis_index("blk"), place.tp, place.y, place.z
+    spot = y * lines + z
+    rows = chunk_rows // (2 * lines)
+    width = gain_ref.shape[-1]
+    wide = query_ref.shape[1]
+    heads = wide // HD
+    span = query_ref.shape[0] // batches
+    per = span // chunk_rows
+    scale = 1.0 / math.sqrt(HD)
+    s3, s4 = Scatter(place, cut, *rest[0:7]), Scatter(place, cut, *rest[7:14])
+    a3 = Gather(place, cut, lambda c: own_mixed.at[c], mixed_hbm, *rest[14:17])
+    a4 = Gather(place, cut, lambda c: own_in.at[c], in_hbm, *rest[17:20])
+
+    get_x = pltpu.make_async_copy(tokens_hbm.at[:, spot], x_own, sem_in)
+    get_x.start()
+
+    def get_kv(step):
+        m, keys = step // (blk + 1), pl.ds(pl.multiple_of(step % (blk + 1) * span, span), span)
+        return (
+            pltpu.make_async_copy(keys_hbm.at[m, keys], key_mb.at[step % 2], sem_kv.at[0, step % 2]),
+            pltpu.make_async_copy(values_hbm.at[m, keys], value_mb.at[step % 2], sem_kv.at[1, step % 2]),
+        )
+
+    def get_feed(c):
+        return pltpu.make_async_copy(feed_hbm.at[c], s3.part.at[c], sem_feed.at[c])
+
+    @pl.loop(0, chunks)
+    def _(c):
+        get_feed(c).start()
+
+    for copy in get_kv(0):
+        copy.start()
+    greet("tp", "blk")
+    get_x.wait()
+    small[...] = jnp.zeros_like(small)
+    small[1:3, :] = sums_ref[...]
+
+    def slab(m):
+        return pl.ds(pl.multiple_of(m * span, span), span)
+
+    ring = stage.shape[0]
+
+    def to_owner(m, k):
+        slot = (m * blk + k) % ring
+        return remote(
+            stage.at[slot], came.at[m % 2, blk], sem_send.at[slot], sem_recv.at[m % 2, blk], (k, tp)
+        )
+
+    def from_peer(m, k):
+        return remote(stage.at[0], came.at[m % 2, k], sem_send.at[0], sem_recv.at[m % 2, k], (k, tp))
+
+    def attend_back(m):
+        here = slab(m)
+        grad = dot_nt(branch_ref[here, :], wo_ref[...]).astype(jnp.bfloat16)
+        for h in range(heads):
+            cols = slice(h * HD, (h + 1) * HD)
+            head = tp * heads + h
+            masked = jnp.where(head < count_ref[here, :], grad[:, cols].astype(jnp.float32), 0.0)
+            grad_mb[:, cols] = masked.astype(jnp.bfloat16)
+            delta = jnp.sum(masked * heads_ref[here, cols].astype(jnp.float32), axis=-1, keepdims=True)
+            delta_mb[h] = jnp.broadcast_to(delta, (span, LANE))
+        dq_mb[...] = jnp.zeros_like(dq_mb)
+        q_rows = blk * span + lax.broadcasted_iota(jnp.int32, (span, span), 0)
+        begin = begin_ref[here, :]
+
+        def pairs(k, out):
+            step = m * (blk + 1) + k
+            for copy in get_kv(step):
+                copy.wait()
+
+            @pl.when(step + 1 < batches * (blk + 1))
+            def _():
+                for copy in get_kv(step + 1):
+                    copy.start()
+
+            k_rows = k * span + lax.broadcasted_iota(jnp.int32, (span, span), 1)
+            allowed = (k_rows <= q_rows) & (k_rows >= begin)
+            for h in range(heads):
+                cols = slice(h * HD, (h + 1) * HD)
+                q, g = query_ref[here, cols], grad_mb[:, cols]
+                key, value = key_mb[step % 2, :, cols], value_mb[step % 2, :, cols]
+                raw = dot_nt(q, key)
+                prob = jnp.where(allowed, jnp.exp(raw * scale - lse_ref[here, h : h + 1]), 0.0)
+                grad_prob = dot_nt(g, value)
+                grad_score = (prob * (grad_prob - delta_mb[h][:, 0:1]) * scale).astype(jnp.bfloat16)
+                dq_mb[:, cols] += dot_nn(grad_score, key)
+                out[:, cols] = dot_tn(grad_score, q).astype(jnp.bfloat16)
+                out[:, wide + h * HD : wide + (h + 1) * HD] = dot_tn(prob.astype(jnp.bfloat16), g).astype(
+                    jnp.bfloat16
+                )
+
+        @pl.loop(0, blk)
+        def _(k):
+            sent = m * blk + k
+
+            @pl.when(sent >= ring)
+            def _():
+                to_owner((sent - ring) // blk, (sent - ring) % blk).wait_send()
+
+            pairs(k, stage.at[sent % ring])
+
+            @pl.when(m >= 2)
+            def _():
+                pl.semaphore_wait(sem_free.at[k], 1)
+
+            to_owner(m, k).start()
+
+        pairs(blk, own.at[m % 2])
+        for h in range(heads):
+            cols = slice(h * HD, (h + 1) * HD)
+            pre[here, cols] = turn_back(dq_mb[:, cols], cos_ref[here, :], sin_ref[here, :]).astype(
+                jnp.bfloat16
+            )
+
+    def gather_kv(m):
+        here = slab(m)
+        grad_w[...] = own[m % 2].astype(jnp.float32)
+
+        @pl.loop(blk + 1, blocks)
+        def _(k):
+            from_peer(m, k).wait_recv()
+            grad_w[...] += came[m % 2, k].astype(jnp.float32)
+
+            @pl.when(m + 2 < batches)
+            def _():
+                pl.semaphore_signal(sem_free.at[blk], inc=1, device_id=(k, tp), device_id_type=MESH)
+
+        for h in range(heads):
+            cols = slice(h * HD, (h + 1) * HD)
+            pre[here, wide + h * HD : wide + (h + 1) * HD] = turn_back(
+                grad_w[:, cols], cos_ref[here, :], sin_ref[here, :]
+            ).astype(jnp.bfloat16)
+        pre[here, 2 * wide :] = grad_w[:, wide:].astype(jnp.bfloat16)
+
+    def spread(c):
+        here = pl.ds(pl.multiple_of(c * chunk_rows, chunk_rows), chunk_rows)
+
+        @pl.loop(0, width // TILE)
+        def _(i):
+            cols = pl.ds(pl.multiple_of(i * TILE, TILE), TILE)
+            grad = dot_nt(pre[here, :wide], wq_ref[cols, :])
+            grad += dot_nt(pre[here, wide : 2 * wide], wk_ref[cols, :])
+            grad += dot_nt(pre[here, 2 * wide :], wv_ref[cols, :])
+            s4.part[c, :, :, :, cols] = grad.astype(jnp.bfloat16).reshape(2, lines, rows, TILE)
+
+        s4.step0(c)
+
+    def feed(c):
+        get_feed(c).wait()
+        s3.step0(c)
+
+    def mix(c):
+        s3.finish(c, total)
+        prob = prob_ref[pl.ds(pl.multiple_of(c * chunk_rows + spot * rows, rows), rows), :]
+        own_mixed[c] = (input_ref[c] + prob * total[...]).astype(jnp.bfloat16)
+        a3.step0(c)
+
+    def last(c):
+        s4.finish(c, total)
+        grad_normed, x = total[...], x_own[c].astype(jnp.float32)
+        inv_rms = lax.rsqrt(mean_last(x * x) + EPS)
+        scaled = x * inv_rms
+        small[0:1, :] += rows_sum(grad_normed * scaled)
+        s = grad_normed * gain_ref[...]
+        grad_in = resid_ref[c] + inv_rms * (s - scaled * mean_last(s * scaled))
+        own_in[c] = grad_in.astype(jnp.bfloat16)
+        a4.step0(c)
+
+    share = width // blocks
+
+    def slice_of(target, out):
+        step = min(TILE, share)
+
+        @pl.loop(0, share // step)
+        def _(i):
+            lanes = pl.ds(pl.multiple_of(target * share + i * step, step), step)
+            out[pl.ds(pl.multiple_of(i * step, step), step), :] = dot_tn(
+                normed_ref[:, lanes], pre[...]
+            ).astype(jnp.bfloat16)
+
+    def out_slice(target, out):
+        lanes = pl.ds(pl.multiple_of(target * share, share), share)
+        out[...] = dot_tn(heads_ref[...], branch_ref[:, lanes]).astype(jnp.bfloat16)
+
+    weights = BlockScatter(blocks, slice_of, *rest[20:25])
+    w_out = rest[25]
+    out_weights = BlockScatter(blocks, out_slice, *rest[26:31])
+    ranks = 2 * lines
+
+    def small_to_blk(k):
+        peer = (blk + k) % blocks
+        lanes = pl.ds(pl.multiple_of(peer * share, share), share)
+        return remote(
+            small.at[:, lanes], small_blk.at[k - 1], sem_blk.at[0, k], sem_blk.at[1, k], (peer, tp)
+        )
+
+    def small_to_tp(k):
+        return remote(
+            small_part, small_tp.at[k - 1], sem_tp.at[0, k], sem_tp.at[1, k], (blk, (tp + k) % ranks)
+        )
+
+    def small_first():
+        for k in range(1, blocks):
+            small_to_blk(k).start()
+
+    def small_second():
+        small_part[...] = small[:, pl.ds(pl.multiple_of(blk * share, share), share)]
+        for k in range(1, blocks):
+            small_to_blk(k).wait()
+            small_part[...] += small_blk[k - 1]
+        for k in range(1, ranks):
+            small_to_tp(k).start()
+
+    def small_third():
+        small_ref[...] = small_part[...]
+        for k in range(1, ranks):
+            small_to_tp(k).wait()
+            small_ref[...] += small_tp[k - 1]
+
+    pre_done = batches * per + 2
+
+    @pl.loop(0, batches * per + 2 + 2 * lines + 1)
+    def _(r):
+        def at(offset, task):
+            c = r - offset
+
+            @pl.when((c >= 0) & (c < chunks))
+            def _():
+                task(c)
+
+        def at_batch(offset, task):
+            c = r - offset
+
+            @pl.when((c >= 0) & (c < chunks) & (c % per == 0))
+            def _():
+                task(c // per)
+
+        for k in range(1, lines):
+            at(k, lambda c, k=k: s3.step(c, k, total_b))
+        for k in range(1, lines):
+            at(2 + k, lambda c, k=k: s4.step(c, k, total_b))
+        for k in range(1, lines + 1):
+            at(lines + k, lambda c, k=k: a3.step(c, k))
+        for k in range(1, lines + 1):
+            at(2 + lines + k, lambda c, k=k: a4.step(c, k))
+        at(2 + lines, last)
+        at(lines, mix)
+        at(0, feed)
+        at_batch(2, gather_kv)
+        at(2, spread)
+        at_batch(0, attend_back)
+
+        pl.when(r == 0)(out_weights.all_first)
+        pl.when(r == 1)(out_weights.all_second)
+        pl.when(r == pre_done)(weights.all_first)
+        pl.when(r == pre_done + 1)(weights.all_second)
+        pl.when(r == chunks + 2 + lines)(small_first)
+        pl.when(r == chunks + 3 + lines)(small_second)
+        pl.when(r == chunks + 5 + lines)(small_third)
+
+    out_weights.third(go_ref)
+    weights.third(w_out)
+    gq_ref[...] = w_out[:, :wide]
+    gk_ref[...] = w_out[:, wide : 2 * wide]
+    gv_ref[...] = w_out[:, 2 * wide :]
+
+    @pl.loop(0, chunks)
+    def _(c):
+        for part in (s3, s4, a3, a4):
+            part.drain(c)
+
+    @pl.loop(jnp.maximum(batches * blk - ring, 0), batches * blk)
+    def _(sent):
+        to_owner(sent // blk, sent % blk).wait_send()
+
+    weights.drain()
+    out_weights.drain()
+
+
+def back(tokens, keys, values, feed_part, own_input, own_resid, grad_branch, query, heads_out, normed, w_query, w_key, w_value, w_out,
+         norm_gain, lse, begin, head_count, router_prob, cos_rows, sin_rows, ln_sums):
+    lines, blocks = lax.axis_size("tp") // 2, lax.axis_size("blk")
+    count, width = tokens.shape
+    batches, key_count, wide = keys.shape
+    chunk_rows = CHUNK_ROWS
+    chunks, rows = count // chunk_rows, chunk_rows // (2 * lines)
+    cut = CUT
+    span = count // batches
+    heads = wide // HD
+    share = width // blocks
+    any_space, vmem = pl.BlockSpec(memory_space=pl.ANY), pl.BlockSpec(memory_space=VMEM)
+    bf16, f32 = jnp.bfloat16, jnp.float32
+    dma = pltpu.SemaphoreType.DMA
+    full = (chunks, 2, lines, rows, width)
+    outs = pl.pallas_call(
+        functools.partial(back_kernel, lines, blocks, batches, chunks, cut, chunk_rows),
+        out_shape=[jax.ShapeDtypeStruct(full, bf16)] * 2
+        + [jax.ShapeDtypeStruct((share, wide), f32)] * 3
+        + [jax.ShapeDtypeStruct((wide, share), f32), jax.ShapeDtypeStruct((8, share), f32)],
+        in_specs=[any_space] * 4 + [vmem] * 18,
+        out_specs=[any_space] * 2 + [vmem] * 5,
+        scratch_shapes=[
+            VMEM((chunks, rows, width), bf16),
+            VMEM((chunks, rows, width), bf16),
+            VMEM((chunks, rows, width), bf16),
+            VMEM((2, span, wide), bf16),
+            VMEM((2, span, wide), bf16),
+            VMEM((span, wide), bf16),
+            VMEM((heads, span, LANE), f32),
+            VMEM((span, wide), f32),
+            VMEM((RING, span, 2 * wide), bf16),
+            VMEM((2, span, 2 * wide), bf16),
+            VMEM((2, blocks, span, 2 * wide), bf16),
+            VMEM((count, 3 * wide), bf16),
+            VMEM((rows, width), f32),
+            VMEM((2, rows, width - cut), f32),
+            VMEM((span, 2 * wide), f32),
+            VMEM((8, width), f32),
+            VMEM((blocks - 1, 8, share), f32),
+            VMEM((8, share), f32),
+            VMEM((2 * lines - 1, 8, share), f32),
+            dma(()),
+            dma((chunks,)),
+            dma((2, 2)),
+            dma((RING,)),
+            dma((2, blocks)),
+            pltpu.SemaphoreType.REGULAR((blocks,)),
+            dma((2, blocks)),
+            dma((2, 2 * lines)),
+        ]
+        + (Scatter.scratch(chunks, lines, rows, width, cut) + Scatter.semaphores(chunks, lines)) * 2
+        + Gather.scratch(chunks, lines) * 2
+        + BlockScatter.scratch(blocks, (share, 3 * wide))
+        + [VMEM((share, 3 * wide), f32)]
+        + BlockScatter.scratch(blocks, (wide, share)),
+        compiler_params=pltpu.CompilerParams(
+            collective_id=2, has_side_effects=True, vmem_limit_bytes=VMEM_LIMIT
+        ),
+        cost_estimate=pl.CostEstimate(
+            flops=2 * count * width * wide * 7, bytes_accessed=40 * 2**20, transcendentals=0
+        ),
+    )(
+        tokens.reshape(chunks, 2 * lines, rows, width), keys, values, feed_part, own_input, own_resid, grad_branch, query,
+        heads_out, normed, w_query, w_key, w_value, w_out, norm_gain[None], lse, begin.reshape(count, 1),
+        head_count.reshape(count, 1), router_prob.reshape(count, 1), cos_rows, sin_rows, ln_sums,
     )
-
-
-def as_sent(array):
-    return jax.tree.map(lambda a: a.astype(jnp.bfloat16) if a.dtype == jnp.float32 else a, array)
+    return outs
 
 
 def seq_begin(lengths, rows):
@@ -625,51 +1123,10 @@
     )
 
 
-def rotate_back(grad_rot, cos_table, sine_table):
-    half_dim = grad_rot.shape[-1] // 2
-    first_half = grad_rot[..., :half_dim]
-    second_half = grad_rot[..., half_dim:]
-    return jnp.concatenate(
-        [
-            first_half * cos_table + second_half * sine_table,
-            second_half * cos_table - first_half * sine_table,
-        ],
-        axis=-1,
-    )
-
-
 def allowed_pairs(q_rows, q_begin, k_rows):
     causal_ok = k_rows[None, None, :] <= q_rows[None, :, None]
     inside_seq = k_rows[None, None, :] >= q_begin[:, :, None]
     return (causal_ok & inside_seq)[:, None]
-
-
-def pair_grads(
-    q_block, grad_block, logsum, row_delta, q_rows, q_begin, k_block, v_block, k_rows, score_scale
-):
-    raw_score = jnp.einsum("mqhd,mkhd->mhqk", q_block, k_block, preferred_element_type=jnp.float32)
-    allowed = allowed_pairs(q_rows, q_begin, k_rows)
-    prob_rows = jnp.where(allowed, jnp.exp(raw_score * score_scale - logsum[..., None]), 0.0)
-    grad_prob = jnp.einsum(
-        "mqhd,mkhd->mhqk", grad_block, v_block, preferred_element_type=jnp.float32
-    )
-    grad_score = (prob_rows * (grad_prob - row_delta[..., None]) * score_scale).astype(jnp.bfloat16)
-    result = []
-    result.append(
-        jnp.einsum("mhqk,mkhd->mqhd", grad_score, k_block, preferred_element_type=jnp.float32)
-    )
-    result.append(
-        jnp.einsum("mhqk,mqhd->mkhd", grad_score, q_block, preferred_element_type=jnp.float32)
-    )
-    result.append(
-        jnp.einsum(
-            "mhqk,mqhd->mkhd",
-            prob_rows.astype(jnp.bfloat16),
-            grad_block,
-            preferred_element_type=jnp.float32,
-        )
-    )
-    return tuple(result)
 
 
 def local(
@@ -701,10 +1158,6 @@
     score_scale = 1.0 / math.sqrt(HD)
     head_ids = lax.axis_index("tp") * local_heads + jnp.arange(local_heads, dtype=jnp.int32)
     head_mask = (head_ids[None, None, :] < head_count[:, :, None]).astype(jnp.float32)
-    unit_ids = lax.axis_index("tp") * unit_count + jnp.arange(unit_count, dtype=jnp.int32)
-    unit_mask = (unit_ids[None, None, :] < (width_index[:, :, None] + 1) * (FF // 4)).astype(
-        jnp.float32
-    )
     block_shape = (batches, rows_dev, local_heads, HD)
     inputs = tokens.astype(jnp.float32)
     inv_rms = lax.rsqrt(jnp.mean(inputs * inputs, axis=-1, keepdims=True) + EPS)
@@ -752,13 +1205,12 @@
     logsum = row_max + jnp.log(row_sum)
     attended = jnp.transpose(weighted / row_sum[..., None], (0, 2, 1, 3)) * head_mask[..., None]
     heads_out = attended.astype(jnp.bfloat16).reshape(batches, rows_dev, local_heads * HD)
-    router_col = router_prob[..., None]
-    upstream = grad_out.astype(jnp.float32)
     count = batches * rows_dev
-    mixed_out, grad_branch, lifted, squared, grad_hidden, own_resid, ln_sums = middle(
+    wide = local_heads * HD
+    grad_branch, feed_part, own_input, own_resid, ln_sums, grad_upw, grad_down = middle(
         tokens.reshape(count, features),
         grad_out.reshape(count, features),
-        heads_out.reshape(count, -1),
+        heads_out.reshape(count, wide),
         w_out,
         ln_gain,
         ln_bias,
@@ -767,122 +1219,44 @@
         router_prob,
         width_index,
     )
-    mixed_out = mixed_out.reshape(tokens.shape)
-    grad_branch = grad_branch.reshape(tokens.shape)
-    grad_feed = (router_col * upstream).astype(jnp.bfloat16).reshape(count, features)
-    grad_down = jnp.einsum("tf,td->fd", squared, grad_feed, preferred_element_type=jnp.float32)
-    grad_upw = jnp.einsum("td,tf->df", lifted, grad_hidden, preferred_element_type=jnp.float32)
-    grad_outw = jnp.einsum(
-        "mte,mtd->ed", heads_out, grad_branch, preferred_element_type=jnp.float32
+    cos_rows = jnp.concatenate([cos_table, cos_table], axis=-1).reshape(count, HD)
+    sin_rows = jnp.concatenate([-sine_table, sine_table], axis=-1).reshape(count, HD)
+    mixed_out, grad_in, grad_wq, grad_wk, grad_wv, grad_outw, sums = back(
+        tokens.reshape(count, features),
+        key_piece.reshape(batches, -1, wide),
+        value_piece.reshape(batches, -1, wide),
+        feed_part,
+        own_input,
+        own_resid,
+        grad_branch,
+        query_local.reshape(count, wide),
+        heads_out.reshape(count, wide),
+        normed.reshape(count, features),
+        w_query,
+        w_key,
+        w_value,
+        w_out,
+        norm_gain,
+        jnp.transpose(logsum, (0, 2, 1)).reshape(count, local_heads),
+        local_begin,
+        head_count,
+        router_prob,
+        cos_rows,
+        sin_rows,
+        ln_sums,
     )
-    grad_heads = (
-        jnp.einsum("mtd,ed->mte", grad_branch, w_out, preferred_element_type=jnp.float32)
-        .astype(jnp.bfloat16)
-        .reshape(block_shape)
-    )
-    grad_block = grad_heads * head_mask[..., None].astype(jnp.bfloat16)
-    row_delta = jnp.sum(grad_block.astype(jnp.float32) * attended, axis=-1)
-    delta_heads = jnp.transpose(row_delta, (0, 2, 1))
-    key_all, value_all = (
-        lax.all_gather(key_local, "blk", axis=1, tiled=True),
-        lax.all_gather(value_local, "blk", axis=1, tiled=True),
-    )
-
-    def key_step(grad_query, piece_index):
-        row_start = piece_index * rows_dev
-        key_piece = lax.dynamic_slice_in_dim(key_all, row_start, rows_dev, 1)
-        value_piece = lax.dynamic_slice_in_dim(value_all, row_start, rows_dev, 1)
-        k_rows = row_start + jnp.arange(rows_dev, dtype=jnp.int32)
-
-        def key_compute_part(running):
-            pair_parts = pair_grads(
-                query_local,
-                grad_block,
-                logsum,
-                delta_heads,
-                local_rows,
-                local_begin,
-                key_piece,
-                value_piece,
-                k_rows,
-                score_scale,
-            )
-            return (running + pair_parts[0], pair_parts[1:])
-
-        def skip_part(running):
-            zero_block = jnp.zeros(block_shape, jnp.float32)
-            return (running, (zero_block, zero_block))
-
-        return lax.cond(row_start > last_row, skip_part, key_compute_part, grad_query)
-
-    grad_query, key_terms = lax.scan(
-        key_step, jnp.zeros(block_shape, jnp.float32), jnp.arange(blocks, dtype=jnp.int32)
-    )
-    summed_keys, summed_values = jax.tree.map(
-        lambda part: part.astype(jnp.float32),
-        lax.psum_scatter(as_sent(key_terms), "blk", scatter_dimension=0, tiled=True),
-    )
-    grad_keys = summed_keys[0]
-    grad_values = summed_values[0]
-    flat_shape = (batches, rows_dev, local_heads * HD)
-    grad_q_pre = (
-        rotate_back(grad_query, cos_table, sine_table).astype(jnp.bfloat16).reshape(flat_shape)
-    )
-    grad_k_pre = (
-        rotate_back(grad_keys, cos_table, sine_table).astype(jnp.bfloat16).reshape(flat_shape)
-    )
-    grad_v_pre = grad_values.astype(jnp.bfloat16).reshape(flat_shape)
-    grad_wq = jnp.einsum("mtd,mte->de", normed, grad_q_pre, preferred_element_type=jnp.float32)
-    grad_wk = jnp.einsum("mtd,mte->de", normed, grad_k_pre, preferred_element_type=jnp.float32)
-    grad_wv = jnp.einsum("mtd,mte->de", normed, grad_v_pre, preferred_element_type=jnp.float32)
-    normed_part = (
-        jnp.einsum("mte,de->mtd", grad_q_pre, w_query, preferred_element_type=jnp.float32)
-        + jnp.einsum("mte,de->mtd", grad_k_pre, w_key, preferred_element_type=jnp.float32)
-        + jnp.einsum("mte,de->mtd", grad_v_pre, w_value, preferred_element_type=jnp.float32)
-    )
-    ranks = lax.axis_size("tp")
-    tp = lax.axis_index("tp")
-    chunks = own_resid.shape[0]
-    split = (chunks, ranks, own_resid.shape[1], features)
-    grad_normed = lax.psum_scatter(
-        normed_part.astype(jnp.bfloat16)
-        .reshape(chunks, 2, ranks // 2, -1, features)
-        .swapaxes(1, 2)
-        .reshape(split),
-        "tp",
-        scatter_dimension=1,
-    ).astype(jnp.float32)
-
-    def own(array):
-        return lax.dynamic_index_in_dim(array.reshape(split[:-1] + (-1,)), tp % 2 * (ranks // 2) + tp // 2, 1, keepdims=False)
-
-    own_scaled = own(tokens).astype(jnp.float32) * own(inv_rms)
-    gain_part = jnp.sum(grad_normed * own_scaled, axis=(0, 1))
-    grad_scaled = grad_normed * norm_gain
-    grad_input = own_resid + own(inv_rms) * (
-        grad_scaled - own_scaled * jnp.mean(grad_scaled * own_scaled, axis=-1, keepdims=True)
-    )
-    grad_in = lax.all_gather(grad_input.astype(jnp.bfloat16), "tp", axis=1)
-    grad_in = grad_in.reshape(chunks, ranks // 2, 2, -1, features).swapaxes(1, 2).reshape(tokens.shape)
-    sums = lax.psum(jnp.concatenate([gain_part[None], ln_sums]), ("blk", "tp"))
-    sums = lax.dynamic_slice_in_dim(sums, lax.axis_index("blk") * (features // blocks), features // blocks, 1)
-    def share(array, dim):
-        return lax.psum_scatter(
-            array.astype(jnp.bfloat16), "blk", scatter_dimension=dim, tiled=True
-        ).astype(jnp.float32)
-
     return (
-        mixed_out,
-        grad_in,
+        mixed_out.reshape(tokens.shape),
+        grad_in.reshape(tokens.shape),
         sums[0],
-        share(grad_wq, 0),
-        share(grad_wk, 0),
-        share(grad_wv, 0),
-        share(grad_outw, 1),
+        grad_wq,
+        grad_wk,
+        grad_wv,
+        grad_outw,
         sums[1],
         sums[2],
-        share(grad_upw, 0),
-        share(grad_down, 1),
+        grad_upw,
+        grad_down,
     )
 
 

time: 870 us -> 534 us (0.61)
  waiting for transfers between devices: 363 us -> 26 us
  Pallas kernels: 270 us -> 421 us
  matrix products: 79.2 us -> 15.2 us
  blocking collectives: 40.9 us -> 0 us
  other arithmetic: 38.6 us -> 16.4 us
  local copies, waits for them, and re-layouts: 49.3 us -> 32.9 us
    reduce_scatter x9 -> x0, waiting for transfers between devices: 307 us -> none  [the longest x6 192 us: share(): lax.psum_scatter(array.astype(jnp.bfloat16), 'blk', scatter_dimension=dim...]
    pallas_call x0 -> x1, Pallas kernels: none -> 200 us  [back(): pl.pallas_call(functools.partial(back_kernel, lines, blocks, batches, chu...]
    dot_general x15 -> x1, matrix products: 62.1 us -> 3.09 us  [attend_compute_part(): jnp.einsum('mhqk,mkhd->mhqd', weights.astype(jnp.bfloat16), value_piece,...]
    pallas_call x1, Pallas kernels: 270 us -> 221 us  [middle(): pl.pallas_call(functools.partial(middle_kernel, lines, chunks, cut, chunk...]
    psum x1 -> x0, blocking collectives: 40.9 us -> none  [local(): sums = lax.psum(jnp.concatenate([gain_part[None], ln_sums]), ('blk', 'tp'))]
    all_gather x1 -> x0, waiting for transfers between devices: 33.5 us -> none  [local(): grad_in = lax.all_gather(grad_input.astype(jnp.bfloat16), 'tp', axis=1)]
    convert_element_type x9 -> x3, other arithmetic: 18.3 us -> 1.38 us  [the longest x1 1.01 us: local(): normed = (scaled * norm_gain).astype(jnp.bfloat16)]
    dynamic_update_slice x12 -> x0, local copies, waits for them, and re-layouts: 15.8 us -> none  [local(): lax.scan(key_step, jnp.zeros(block_shape, jnp.float32), jnp.arange(blocks...]
  transfers between devices with their start and end apart: 12 -> 2, of which waited for: 11 -> 2; matrix products, arithmetic and copies ran while one was open for 11% -> 4% of each run, Pallas kernels for 0% -> 0%
where the time goes in v2:
time: 534 us; the launch traced here: 527 us
  Pallas kernels  421 us (79%)
  local copies, waits for them, and re-layouts  32.9 us (6%)
  waiting for transfers between devices  26 us (5%)
  other arithmetic  16.4 us (3%)
  matrix products  15.2 us (3%)
  between operations  14.7 us (3%)
    pallas_call x1, Pallas kernels, middle(): pl.pallas_call(functools.partial(middle_kernel, lines, chunks, cut, chunk...  221 us
    pallas_call x1, Pallas kernels, back(): pl.pallas_call(functools.partial(back_kernel, lines, blocks, batches, chu...  200 us
    all_gather x1, waiting for transfers between devices, local(): key_piece = lax.all_gather(key_local, 'blk', axis=1, tiled=True)  24.8 us
    unnamed x61, local copies, waits for them, and re-layouts  24.2 us
  transfers between devices with their start and end apart: 2, of which 2 were waited for; matrix products, arithmetic and copies ran while one was open for 4% of the time, Pallas kernels for 0%

profile of v2, /device:TPU:0, one launch (start us, length us, event | category | flops | bytes accessed | tf_op | source)
XLA Modules:
  0.0 526.7 jit_solution(3200778263697161110)
XLA Ops:
  7.2 0.0 all-gather.5.cloned.1.call-start
  7.2 3.2 fusion.9
  10.5 0.2 copy-done
  10.7 1.0 fusion.11
  11.7 0.0 copy-start.1
  11.7 2.0 copy-done.1
  13.7 1.3 convolution_convert_fusion
  15.0 1.0 copy.54
  16.0 0.0 all-gather.5.cloned.1.call-update
  16.1 0.6 all-gather.3.cloned.1.call-start
  16.7 3.5 fusion.16
  20.1 0.0 copy-start.17
  20.2 0.1 fusion.20
  20.3 0.3 copy.66
  20.6 0.0 copy-start.19
  20.6 0.0 copy-start.16
  20.6 0.3 copy.67
  21.0 0.2 reduce_window_sum.11
  21.2 0.1 select_reduce_fusion
  21.3 1.9 multiply_cosine_fusion.1
  23.2 0.3 subtract_convert_fusion
  23.5 1.1 pad_maximum_fusion
  24.6 0.0 all-gather.3.cloned.1.call-update
  24.7 1.0 copy.81
  25.7 1.0 copy.74
  26.8 1.0 copy.76
  27.8 1.0 copy.79
  28.8 3.5 fusion.13
  32.3 0.9 fusion.19
  33.2 0.3 copy.68
  33.5 1.4 copy.69
  34.9 0.3 multiply_subtract_fusion
  35.2 0.3 maximum_convert_fusion
  35.5 0.5 copy.61
  36.1 0.9 copy.87
  37.0 1.9 fusion.18
  38.9 1.3 pad_maximum_fusion.1
  40.2 0.1 compare_convert_fusion
  40.3 1.2 all-gather.5.cloned.1.call-done
  41.5 24.8 %all-gather.3.cloned.1.call-done = bf16[4,1024,2,128]{3,1,2,0:T(8,128)(2,1)} async-done(((bf16[4,256,2,128]{3,1,2,0:T(8,128)(2,1)}), bf16[4,1024,2,128]{3,1,2,0:T(8,128)(2,1)}) %all-gather.3.cloned.1.call-update) | async-done | bytes 2097168 | tf_op jit(solution)/shard_map/all_gather | solution.py:1180
  66.3 11.1 %conditional.1 = (f32[4,2,256]{2,1,0:T(2,128)S(1)}, f32[4,2,256]{2,1,0:T(2,128)S(1)}, f32[4,2,256,128]{3,2,1,0:T(8,128)S(1)}, f32[4,2,256]{2,1,0:T(2,128)S(1)}) conditional(s32[]{:T(128)} %convert_element_type.51, (s32[1024]{0:T(1024)S(1)}, s32[]{:T(128)}, s32[256]{0:T(256)S(1)}, s32[1024]{0:T(1024)S(1)}, s32[4,256]{1,0:T(4,128)S(1)}, ...), branch_computations={%region_3.6_spmd, %region_6.7_spmd} | conditional | flops 1103362304 | bytes 44121152 | solution.py:1202
  66.3 0.2 broadcast_compare_fusion
  66.5 0.8 compare_and_fusion
  67.3 3.9 fusion
  71.2 3.1 fusion.3
  74.3 3.1 fusion.2
  77.4 0.6 fusion.12
  78.0 0.5 copy.58
  78.5 0.9 copy.88
  79.4 1.0 copy.62
  80.4 221.3 %shard_map.230 = (bf16[8,2,4,16,2048]{4,3,2,1,0:T(8,128)(2,1)}, bf16[8,2,4,16,2048]{4,3,2,1,0:T(8,128)(2,1)}, f32[8,16,2048]{2,1,0:T(8,128)}, f32[8,16,2048]{2,1...) custom-call(bf16[8,8,16,2048]{3,2,1,0:T(8,128)(2,1)} %bitcast.76, ...), custom_call_target="tpu_custom_call" | custom-call | flops 26843545600 | bytes 41943040 | tf_op jit(solution)/shard_map/pallas_call | solution.py:682
  301.8 1.5 copy_bitcast_fusion.1.keys_hbm
  303.3 0.8 copy-done.4
  304.1 1.5 copy_bitcast_fusion.values_hbm
  305.6 199.6 %shard_map.231 = (bf16[8,2,4,16,2048]{4,3,2,1,0:T(8,128)(2,1)}, bf16[8,2,4,16,2048]{4,3,2,1,0:T(8,128)(2,1)}, f32[512,256]{1,0:T(8,128)}, f32[512,256]{1,0:T(8,1...) custom-call(bf16[8,8,16,2048]{3,2,1,0:T(8,128)(2,1)} %bitcast.77, ...), custom_call_target="tpu_custom_call" | custom-call | flops 7516192768 | bytes 41943040 | tf_op jit(solution)/shard_map/pallas_call | solution.py:1045
  505.3 1.4 fusion.21
  506.7 4.9 copy.105
  511.7 2.1 copy.106
  513.8 0.8 copy.107
  514.6 0.8 copy.108
  515.4 0.8 copy.109
  516.2 0.8 copy.110
  517.0 1.3 copy.111
  518.3 1.3 copy.112
  (51 shorter events, 0.2 us)
Async XLA Ops:
  7.2 3.3 copy-start.15
  7.2 34.3 %all-gather.5.cloned.1.call-start = ((), (), s32[]{:S(2)}) async-start(), calls=%async_computation.1 | async-start | bytes 2621440 | tf_op jit(solution)/shard_map/all_gather | solution.py:1181
  7.2 3.5 copy-start
  10.7 3.0 copy-start.8
  11.7 2.0 copy-start.1
  13.7 2.9 copy-start.9
  16.1 50.2 %all-gather.3.cloned.1.call-start = ((), (), s32[]{:S(2)}) async-start(), calls=%async_computation | async-start | bytes 2621440 | tf_op jit(solution)/shard_map/all_gather | solution.py:1180
  20.1 0.8 copy-start.17
  20.6 4.0 copy-start.18
  20.6 4.0 copy-start.19
  20.6 4.1 copy-start.16
  23.5 5.3 %copy-start.10 = (bf16[2048,256]{1,0:T(8,128)(2,1)S(1)}, bf16[2048,256]{1,0:T(8,128)(2,1)}, u32[]{:S(2)}) copy-start(bf16[2048,256]{1,0:T(8,128)(2,1)} %wq_ref.1) | copy-start | bytes 3145732
  67.3 3.9 copy-start.5
  80.4 221.3 %copy-start.2 = (bf16[4,1024,2,128]{3,1,2,0:T(8,128)(2,1)S(1)}, bf16[4,1024,2,128]{3,1,2,0:T(8,128)(2,1)}, u32[]{:S(2)}) copy-start(bf16[4,1024,2,128]{3,1,2,0:T(8,128)(2,1)} %all-gather.3.cloned.1.call-done) | copy-start | bytes 6291460
  301.7 2.3 copy-start.4
  506.7 4.9 copy-start.3
  511.6 2.2 copy-start.14
  511.6 3.0 copy-start.13
  511.6 3.8 copy-start.12
  511.6 4.6 copy-start.11
  511.7 5.3 %copy-start.7 = (f32[512,1024]{1,0:T(8,128)S(1)}, f32[512,1024]{1,0:T(8,128)}, u32[]{:S(2)}) copy-start(f32[512,1024]{1,0:T(8,128)} %get-tuple-element.121) | copy-start | bytes 6291460
  513.8 4.5 copy-start.6
Sparse Core Ops, SparseCore 0:
  16.2 25.2 all-gather.4
  43.6 22.5 all-gather.2
